TPU v7x, 128 devices: a whole 4x4x4 slice. The times are simulated.
128 devices in a mesh: branch: 8 (over y, core), mp: 16 (over z, x).
Axes of the slice: x: 4, y: 4, z: 4, core: 2. Of those that a mesh axis runs over, the one named last changes fastest.
Arguments:
- tokens: bfloat16 [768, 8192], P('mp'), may hold values from -6 to 6
- cotangent: bfloat16 [768, 8192], P('mp'), may hold values from -6 to 6
- routes: int32 [768, 2], P('mp'), may hold values from 0 to 3, all different within a row; in each aligned block of 48 rows (0 to 47, 48 to 95, ...) at most 30 rows name the same one
- router_gates: float32 [768, 2], P('mp'), may hold values from 0.1 to 0.9
- expert_in: bfloat16 [2, 8192, 57344], P(None, None, ('branch', 'mp')), may hold values from -0.0625 to 0.0625
- expert_down: bfloat16 [57344, 8192], P('branch', 'mp'), may hold values from -0.046875 to 0.046875
Outputs:
- layer_output: bfloat16 [768, 8192], P('mp', 'branch')
- token_grads: bfloat16 [768, 8192], P('mp', 'branch')
Inputs may be any that keep to these rules, and one draw needn't show every extreme that they name: `routes`: each row names 2 different experts. Among the tokens of one index of mp no expert is named more than 30 times, and in every draw some expert is named exactly 30 times there.
All inputs are finite; a program needn't handle non-finite values.
Results may differ from a plain program's by a relative error of at most 0.023.
Values may be sent and summed in bfloat16 or wider, within the bound.
A program may use at most 192 MiB of HBM per device.

v0:
```python
import jax
import jax.numpy as jnp
from jax import lax
from jax.sharding import PartitionSpec as P

EXPERTS = 4
CAP = 30


def pick_table(route_rows, expert, slot_total):
    chosen = jnp.any(route_rows == expert, axis=-1)
    counted = chosen.astype(jnp.int32)
    places = jnp.cumsum(counted) - counted
    slot_ids = jnp.arange(slot_total, dtype=jnp.int32)
    slot_table = jnp.logical_and(slot_ids[:, None] == places[None, :], chosen[None, :])
    return (chosen, places, slot_table.astype(jnp.bfloat16))


def pick_rows(slot_table, values):
    return jnp.dot(slot_table, values, preferred_element_type=jnp.float32).astype(jnp.bfloat16)


def contract_last(left, right):
    return lax.dot_general(
        left, right, (((1,), (1,)), ((), ())), preferred_element_type=jnp.float32
    )


def on_device(tokens, cotangent, routes, router_gates, expert_in, expert_down):
    branches = lax.axis_size("branch")
    shards = lax.axis_size("mp")
    branch_id = lax.axis_index("branch")
    expert = branch_id // (branches // EXPERTS)
    down_block = lax.all_to_all(expert_down, "mp", split_axis=0, concat_axis=1, tiled=True)
    own_chosen, own_places, own_table = pick_table(routes, expert, CAP)
    all_tokens, all_grads = (
        lax.all_gather(tokens, "mp", axis=0, tiled=True),
        lax.all_gather(cotangent, "mp", axis=0, tiled=True),
    )
    all_routes = lax.all_gather(routes, "mp", axis=0, tiled=True)
    per_block = tokens.shape[0]

    def build_slots(route_rows, token_rows, cotangent_rows):
        _, _, slot_table = pick_table(route_rows, expert, CAP)
        return (pick_rows(slot_table, token_rows), pick_rows(slot_table, cotangent_rows))

    inputs, grad_rows = jax.vmap(build_slots)(
        all_routes.reshape(shards, per_block, -1),
        all_tokens.reshape(shards, per_block, -1),
        all_grads.reshape(shards, per_block, -1),
    )
    inputs = inputs.reshape(shards * CAP, -1)
    grad_rows = grad_rows.reshape(shards * CAP, -1)
    gate_block = expert_in[0]
    up_block = expert_in[1]
    pre_gate = jnp.dot(inputs, gate_block, preferred_element_type=jnp.float32)
    pre_up = jnp.dot(inputs, up_block, preferred_element_type=jnp.float32)
    sigmoid_gate = jax.nn.sigmoid(pre_gate)
    active = (pre_gate * sigmoid_gate * pre_up).astype(jnp.bfloat16)
    part_out = jnp.dot(active, down_block, preferred_element_type=jnp.float32)
    back_hidden = contract_last(grad_rows, down_block)
    gate_grad = (
        back_hidden * pre_up * sigmoid_gate * (1.0 + pre_gate * (1.0 - sigmoid_gate))
    ).astype(jnp.bfloat16)
    up_grad = (back_hidden * pre_gate * sigmoid_gate).astype(jnp.bfloat16)
    part_in = contract_last(gate_grad, gate_block) + contract_last(up_grad, up_block)
    slot_out, slot_in = (
        lax.psum_scatter(
            part_out.astype(jnp.bfloat16), "mp", scatter_dimension=0, tiled=True
        ).astype(jnp.float32),
        lax.psum_scatter(
            part_in.astype(jnp.bfloat16), "mp", scatter_dimension=0, tiled=True
        ).astype(jnp.float32),
    )
    expert_gate = jnp.sum(jnp.where(routes == expert, router_gates, 0.0), axis=-1)
    weighting = jnp.where(own_chosen, expert_gate, 0.0)[:, None]
    where_from = jnp.minimum(own_places, CAP - 1)
    token_out = weighting * jnp.take(slot_out, where_from, axis=0)
    token_in = weighting * jnp.take(slot_in, where_from, axis=0)
    final_out, final_in = (
        lax.psum_scatter(
            token_out.astype(jnp.bfloat16), "branch", scatter_dimension=1, tiled=True
        ).astype(jnp.float32),
        lax.psum_scatter(
            token_in.astype(jnp.bfloat16), "branch", scatter_dimension=1, tiled=True
        ).astype(jnp.float32),
    )
    return (final_out.astype(jnp.bfloat16), final_in.astype(jnp.bfloat16))


def solution(mesh):
    placed = (
        P("mp", None),
        P("mp", None),
        P("mp", None),
        P("mp", None),
        P(None, None, ("branch", "mp")),
        P("branch", "mp"),
    )
    return jax.shard_map(
        on_device,
        mesh=mesh,
        in_specs=placed,
        out_specs=(P("mp", "branch"), P("mp", "branch")),
        check_vma=False,
    )
```

profile of v0, /device:TPU:1, one launch (start us, length us, event | category | flops | bytes accessed | tf_op | source)
XLA Modules:
  0.0 632.1 jit_solution(8883454128496423965)
XLA Ops:
  7.2 0.0 all-gather.4.cloned.1.call-start
  7.2 0.7 all-gather.4.cloned.1.call-update
  7.9 0.0 copy-start.5
  7.9 0.0 all-gather.6.cloned.1.call-start
  8.0 0.7 all-gather.6.cloned.1.call-update
  8.7 8.5 %all-to-all-start = ((bf16[16,448,512]{2,1,0:T(8,128)(2,1)}), bf16[16,448,512]{2,1,0:T(8,128)(2,1)}, u32[]{:S(2)}, u32[]{:S(2)}) async-start(bf16[16,448,512]{2,1,0:T(8,128)(2,1)} %bitcast.38), calls=%async_computation | async-start | bytes 14680064 | tf_op jit(solution)/shard_map/all_to_all | solution.py:34
  17.1 0.0 reduce-scatter.7.cloned.1.call-start
  17.2 0.0 copy-done.5
  17.2 138.0 %all-gather = s32[16,48,2]{1,2,0:T(2,128)S(1)} all-gather(s32[1,48,2]{1,2,0:T(2,128)S(1)} %bitcast.39), channel_id=1, replica_groups=mesh['branch'=8,'mp'=16] {'mp'}, dimensions={0}, use_global_device_ids=true | all-gather | bytes 6528 | tf_op jit(solution)/shard_map/all_gather | solution.py:40
  155.3 0.2 reduce_window_sum.18
  155.5 0.1 copy.11
  155.6 0.1 reduce-window.9
  155.7 0.1 reduce.2
  155.8 0.0 all-to-all-done
  155.8 7.1 %copy.13 = bf16[16,56,8,512]{3,2,0,1:T(8,128)(2,1)} copy(bf16[16,56,8,512]{3,2,1,0:T(8,128)(2,1)} %bitcast.13) | data formatting | bytes 14680064 | tf_op jit(solution)/shard_map/all_to_all | solution.py:34
  162.9 24.5 %all-gather.4.cloned.1.call-done = bf16[768,8192]{1,0:T(8,128)(2,1)} async-done(((bf16[48,8192]{1,0:T(8,128)(2,1)}), bf16[768,8192]{1,0:T(8,128)(2,1)}) %all-gather.4.cloned.1.call-update) | async-done | bytes 12582928 | tf_op jit(solution)/shard_map/all_gather | solution.py:37
  187.4 10.1 %convolution_convert_fusion.1 = bf16[16,30,8192]{2,1,0:T(8,128)(2,1)} fusion(bf16[16,48,8192]{2,1,0:T(8,128)(2,1)} %bitcast.33, s32[16,48]{1,0:T(8,128)S(1)} %convert_subtract_fusion, pred[16,48]{1,0:T(8,128)(4,1)S(1)} %compare_reduce_fusion), kind=kOutput, calls=%fused_computation.4 | convolution fusion | flops 381465600 | bytes 20451072 | tf_op jit(solution)/shard_map/vmap()/dot_general | solution.py:20
  197.5 8.1 %reshape.80 = bf16[480,8192]{1,0:T(8,128)(2,1)} reshape(bf16[16,30,8192]{2,1,0:T(8,128)(2,1)} %convolution_convert_fusion.1) | data formatting | bytes 15728640 | tf_op jit(solution)/shard_map/reshape | solution.py:52
  205.6 0.0 copy-start.2
  205.6 10.6 %fusion.3 = f32[480,448]{0,1:T(8,128)} fusion(bf16[480,8192]{1,0:T(8,128)(2,1)} %reshape.80, bf16[2,8192,448]{1,2,0:T(8,128)(2,1)} %param.12), kind=kOutput, calls=%fused_computation.7 | convolution fusion | flops 3523215360 | bytes 16064512 | tf_op jit(solution)/shard_map/dot_general | solution.py:57
  216.2 0.0 copy-done.2
  216.2 7.3 %fusion.7 = f32[480,448]{0,1:T(8,128)} fusion(bf16[480,8192]{1,0:T(8,128)(2,1)S(1)} %copy-done.2, bf16[2,8192,448]{1,2,0:T(8,128)(2,1)} %param.12), kind=kOutput, calls=%fused_computation.11 | convolution fusion | flops 3523215360 | bytes 16064512 | tf_op jit(solution)/shard_map/dot_general | solution.py:56
  223.5 54.7 %all-gather.6.cloned.1.call-done = bf16[768,8192]{1,0:T(8,128)(2,1)} async-done(((bf16[48,8192]{1,0:T(8,128)(2,1)}), bf16[768,8192]{1,0:T(8,128)(2,1)}) %all-gather.6.cloned.1.call-update) | async-done | bytes 12582928 | tf_op jit(solution)/shard_map/all_gather | solution.py:38
  278.2 10.1 %convolution_convert_fusion = bf16[16,30,8192]{2,1,0:T(8,128)(2,1)} fusion(bf16[16,48,8192]{2,1,0:T(8,128)(2,1)} %bitcast.32, s32[16,48]{1,0:T(8,128)S(1)} %convert_subtract_fusion, pred[16,48]{1,0:T(8,128)(4,1)S(1)} %compare_reduce_fusion), kind=kOutput, calls=%fused_computation.3 | convolution fusion | flops 381465600 | bytes 20451072 | tf_op jit(solution)/shard_map/vmap()/dot_general | solution.py:20
  288.3 0.0 slice-start
  288.3 7.9 %reshape.83 = bf16[480,8192]{1,0:T(8,128)(2,1)} reshape(bf16[16,30,8192]{2,1,0:T(8,128)(2,1)} %convolution_convert_fusion) | data formatting | bytes 15728640 | tf_op jit(solution)/shard_map/reshape | solution.py:53
  296.3 0.0 slice-start.1
  296.3 0.0 copy-start
  296.3 0.0 copy-start.3
  296.3 9.0 %fusion.31 = f32[480,448]{0,1:T(8,128)S(1)} fusion(bf16[480,8192]{1,0:T(8,128)(2,1)} %reshape.83, bf16[448,8192]{1,0:T(8,128)(2,1)} %bitcast.34), kind=kOutput, calls=%fused_computation.51 | convolution fusion | flops 3523215360 | bytes 16064512 | tf_op jit(solution)/shard_map/dot_general | solution.py:24
  305.3 0.0 slice-done
  305.3 0.0 slice-done.1
  305.3 0.0 copy-done
  305.3 0.0 copy-done.3
  305.3 0.0 copy-start.4
  305.3 6.8 %convolution_convert_fusion.2 = bf16[480,8192]{1,0:T(8,128)(2,1)} fusion(bf16[448,8192]{1,0:T(8,128)(2,1)S(1)} %bitcast.37, f32[480,448]{0,1:T(8,128)S(1)} %copy-done.3, f32[480,448]{0,1:T(8,128)S(1)} %copy-done), kind=kOutput, calls=%fused_computation.5 | convolution fusion | flops 3528437760 | bytes 16924672 | tf_op jit(solution)/shard_map/dot_general | solution.py:60
  312.2 0.0 copy-done.4
  312.2 0.0 copy-start.1
  312.2 11.2 %fusion.5 = f32[480,8192]{1,0:T(8,128)} fusion(bf16[2,8192,448]{1,2,0:T(8,128)(2,1)} %param.12, f32[480,448]{0,1:T(8,128)S(1)} %copy-done, f32[480,448]{0,1:T(8,128)S(1)} %fusion.31, f32[480,448]{0,1:T(8,128)S(1)} %copy-done.3), kind=kOutput, calls=%fused_computation.9 | convolution fusion | flops 3525365760 | bytes 25649152 | tf_op jit(solution)/shard_map/dot_general | solution.py:24
  323.4 0.0 copy-done.1
  323.4 15.4 %add_convert_fusion = bf16[480,8192]{1,0:T(8,128)(2,1)} fusion(f32[480,8192]{1,0:T(8,128)} %fusion.5, bf16[2,8192,448]{1,2,0:T(8,128)(2,1)} %param.12, f32[480,448]{0,1:T(8,128)} %copy-done.4, f32[480,448]{0,1:T(8,128)S(1)} %copy-done.1), kind=kOutput, calls=%fused_computation.2 | convolution fusion | flops 3532369920 | bytes 32710656 | tf_op jit(solution)/shard_map/dot_general | solution.py:24
  338.7 0.0 copy-start.7
  338.7 187.9 %fusion.30 = (bf16[32,8192]{1,0:T(8,128)(2,1)S(1)}, bf16[32,8192]{1,0:T(8,128)(2,1)S(1)}) fusion(bf16[480,8192]{1,0:T(8,128)(2,1)} %convolution_convert_fusion.2, bf16[480,8192]{1,0:T(8,128)(2,1)} %add_convert_fusion), kind=kCustom, calls=%all-reduce-scatter.2 | all-reduce-scatter fusion | flops 8388609 | bytes 16777728
  526.6 0.1 slice.12
  526.8 2.1 collective-permute-start
  528.9 0.0 copy-done.7
  528.9 0.6 dynamic-slice.6
  530.1 0.0 copy-done.6
  530.2 0.1 slice.13
  530.3 2.1 collective-permute-start.1
  532.4 5.3 collective-permute-done
  537.7 2.9 concatenate
  540.6 0.1 dynamic-slice_convert_fusion.1
  540.8 8.2 %collective-permute-done.1 = bf16[30,8192]{1,0:T(8,128)(2,1)} collective-permute-done((bf16[30,8192]{1,0:T(8,128)(2,1)S(1)}, bf16[30,8192]{1,0:T(8,128)(2,1)}, u32[]{:S(2)}, u32[]{:S(2)}) %collective-permute-start.1) | collective-permute-done | bytes 491552
  549.0 2.9 concatenate.1
  551.9 0.1 dynamic-slice_convert_fusion
  552.0 2.1 gather_fusion
  554.2 2.2 gather_fusion.1
  556.3 3.4 fusion.13
  559.7 0.0 reduce-scatter.7.cloned.1.call-update
  559.7 0.0 reduce-scatter.9.cloned.1.call-start
  559.8 0.5 reduce-scatter.9.cloned.1.call-update
  560.3 32.1 %reduce-scatter.7.cloned.1.call-done = bf16[48,1024]{1,0:T(8,128)(2,1)} async-done(((bf16[48,8192]{1,0:T(8,128)(2,1)}), bf16[48,1024]{1,0:T(8,128)(2,1)}) %reduce-scatter.7.cloned.1.call-update) | async-done | bytes 98320 | tf_op jit(solution)/shard_map/reduce_scatter | solution.py:81
  592.4 33.2 %reduce-scatter.9.cloned.1.call-done = bf16[48,1024]{1,0:T(8,128)(2,1)} async-done(((bf16[48,8192]{1,0:T(8,128)(2,1)}), bf16[48,1024]{1,0:T(8,128)(2,1)}) %reduce-scatter.9.cloned.1.call-update) | async-done | bytes 98320 | tf_op jit(solution)/shard_map/reduce_scatter | solution.py:84
  (11 shorter events, 0.1 us)
Async XLA Ops:
  7.2 180.2 %all-gather.4.cloned.1.call-start = ((), (), s32[]{:S(2)}) async-start(), calls=%async_computation.3 | async-start | bytes 13369344 | tf_op jit(solution)/shard_map/all_gather | solution.py:37
  7.9 9.3 %copy-start.5 = (s32[48,2]{0,1:T(2,128)S(1)}, s32[48,2]{0,1:T(2,128)}, u32[]{:S(2)}) copy-start(s32[48,2]{0,1:T(2,128)} %param.10) | copy-start | bytes 1156
  7.9 270.3 %all-gather.6.cloned.1.call-start = ((), (), s32[]{:S(2)}) async-start(), calls=%async_computation.5 | async-start | bytes 13369344 | tf_op jit(solution)/shard_map/all_gather | solution.py:38
  8.7 147.2 %all-to-all-start = ((bf16[16,448,512]{2,1,0:T(8,128)(2,1)}), bf16[16,448,512]{2,1,0:T(8,128)(2,1)}, u32[]{:S(2)}, u32[]{:S(2)}) async-start(bf16[16,448,512]{2,1,0:T(8,128)(2,1)} %bitcast.38), calls=%async_computation | async-start | bytes 14680064 | tf_op jit(solution)/shard_map/all_to_all | solution.py:34
  17.1 575.3 %reduce-scatter.7.cloned.1.call-start = ((), (), s32[]{:S(2)}) async-start(), calls=%async_computation.4 | async-start | bytes 884736 | tf_op jit(solution)/shard_map/reduce_scatter | solution.py:81
  205.6 10.7 %copy-start.2 = (bf16[480,8192]{1,0:T(8,128)(2,1)S(1)}, bf16[480,8192]{1,0:T(8,128)(2,1)}, u32[]{:S(2)}) copy-start(bf16[480,8192]{1,0:T(8,128)(2,1)} %reshape.80) | copy-start | bytes 23592964
  288.3 17.0 %slice-start = ((s8[7340032]{0:T(1024)(128)(4,1)}), s8[3145728]{0:T(1024)(128)(4,1)S(1)}, s32[]{:S(2)}) async-start(s8[7340032]{0:T(1024)(128)(4,1)} %bitcast.35), calls=%async_computation.7 | async-start | bytes 6291456
  296.3 9.0 %slice-start.1 = ((s8[7340032]{0:T(1024)(128)(4,1)}), s8[4194304]{0:T(1024)(128)(4,1)S(1)}, s32[]{:S(2)}) async-start(s8[7340032]{0:T(1024)(128)(4,1)} %bitcast.35), calls=%async_computation.8 | async-start | bytes 8388608
  296.3 9.0 %copy-start = (f32[480,448]{0,1:T(8,128)S(1)}, f32[480,448]{0,1:T(8,128)}, u32[]{:S(2)}) copy-start(f32[480,448]{0,1:T(8,128)} %fusion.7) | copy-start | bytes 2580484
  296.3 9.1 %copy-start.3 = (f32[480,448]{0,1:T(8,128)S(1)}, f32[480,448]{0,1:T(8,128)}, u32[]{:S(2)}) copy-start(f32[480,448]{0,1:T(8,128)} %fusion.3) | copy-start | bytes 2580484
  305.3 6.9 %copy-start.4 = (f32[480,448]{0,1:T(8,128)}, f32[480,448]{0,1:T(8,128)S(1)}, u32[]{:S(2)}) copy-start(f32[480,448]{0,1:T(8,128)S(1)} %fusion.31) | copy-start | bytes 2580484
  312.2 11.2 %copy-start.1 = (f32[480,448]{0,1:T(8,128)S(1)}, f32[480,448]{0,1:T(8,128)}, u32[]{:S(2)}) copy-start(f32[480,448]{0,1:T(8,128)} %fusion.7) | copy-start | bytes 2580484
  338.7 190.1 %copy-start.7 = (u32[128]{0:T(128)S(1)}, u32[128]{0:T(128)}, u32[]{:S(2)}) copy-start(u32[128]{0:T(128)} %constant.47) | copy-start | bytes 1540
  338.7 191.4 %copy-start.6 = (f32[48,2]{0,1:T(2,128)S(1)}, f32[48,2]{0,1:T(2,128)}, u32[]{:S(2)}) copy-start(f32[48,2]{0,1:T(2,128)} %param.11) | copy-start | bytes 1156
  526.8 11.0 %collective-permute-start = (bf16[30,8192]{1,0:T(8,128)(2,1)S(1)}, bf16[30,8192]{1,0:T(8,128)(2,1)}, u32[]{:S(2)}, u32[]{:S(2)}) collective-permute-start(bf16[30,8192]{1,0:T(8,128)(2,1)S(1)} %slice.12), channel_id=1, source_target_pairs={{0,1},{1,2},{2,3},{3,4},{4,5},{5,6},{6,7},{7,8},{8,9},{9,10},{10,1... | collective-permute-start | bytes 1474568
  530.3 18.7 %collective-permute-start.1 = (bf16[30,8192]{1,0:T(8,128)(2,1)S(1)}, bf16[30,8192]{1,0:T(8,128)(2,1)}, u32[]{:S(2)}, u32[]{:S(2)}) collective-permute-start(bf16[30,8192]{1,0:T(8,128)(2,1)S(1)} %slice.13), channel_id=1, source_target_pairs={{0,1},{1,2},{2,3},{3,4},{4,5},{5,6},{6,7},{7,8},{8,9},{9,10},{10,1... | collective-permute-start | bytes 1474568
  559.7 65.8 %reduce-scatter.9.cloned.1.call-start = ((), (), s32[]{:S(2)}) async-start(), calls=%async_computation.6 | async-start | bytes 884736 | tf_op jit(solution)/shard_map/reduce_scatter | solution.py:84
Sparse Core Ops, SparseCore 0:
  10.1 177.2 all-gather.3
  189.5 88.6 all-gather.5
  559.8 32.5 reduce-scatter.6
  595.4 30.1 reduce-scatter.8
where the time goes:
time: 635 us; the launch traced here: 632 us
  blocking collectives  326 us (51%)
  waiting for transfers between devices  160 us (25%)
  matrix products  80.5 us (13%)
  local copies, waits for them, and re-layouts  34.1 us (5%)
  between operations  14.6 us (2%)
  starting transfers between devices  12.8 us (2%)
    unnamed x1, blocking collectives  188 us
    all_gather x1, blocking collectives, on_device(): all_routes = lax.all_gather(routes, 'mp', axis=0, tiled=True)  138 us
    all_gather x1, waiting for transfers between devices, on_device(): lax.all_gather(cotangent, 'mp', axis=0, tiled=True)  54.7 us
    dot_general x3, matrix products, contract_last(): lax.dot_general(left, right, (((1,), (1,)), ((), ())), preferred_element_...  35.5 us
    reduce_scatter x1, waiting for transfers between devices, on_device(): lax.psum_scatter(token_in.astype(jnp.bfloat16), 'branch', scatter_dimensi...  33.2 us
    reduce_scatter x1, waiting for transfers between devices, on_device(): lax.psum_scatter(token_out.astype(jnp.bfloat16), 'branch', scatter_dimens...  32.1 us
    all_gather x1, waiting for transfers between devices, on_device(): lax.all_gather(tokens, 'mp', axis=0, tiled=True)  24.5 us
    dot_general x2, matrix products, pick_rows(): jnp.dot(slot_table, values, preferred_element_type=jnp.float32)  20.2 us
  transfers between devices with their start and end apart: 7, of which 6 were waited for; matrix products, arithmetic and copies ran while one was open for 8% of the time, Pallas kernels for 0%

commit v1 on v0

v1 whole, which is shorter than its diff:
```python
import functools

import jax
import jax.numpy as jnp
from jax import lax
from jax.experimental import pallas as pl
from jax.experimental.pallas import tpu as pltpu
from jax.sharding import PartitionSpec as P

MESH = pl.DeviceIdType.MESH
BF = jnp.bfloat16
F32 = jnp.float32

EXPERTS = 4
NB = 8
NM = 16
TOK = 48
D = 8192
HID = 448
MAIN, TAIL = 384, 64
CH = 2 * HID
SLOTS = 15
PAD = 16
ROWS = SLOTS * NM
PROWS = PAD * NM
COLS = D // NM
OUTC = D // NB
KC = 512
NK = D // KC
WB = 3
HALF0 = 128


def dot(a, b):
    return jnp.dot(a, b, preferred_element_type=F32)


def dot_nt(a, b):
    return lax.dot_general(a, b, (((1,), (1,)), ((), ())), preferred_element_type=F32)


def to_slot_major():
    q = lax.broadcasted_iota(jnp.int32, (ROWS, PROWS), 0)
    r = lax.broadcasted_iota(jnp.int32, (ROWS, PROWS), 1)
    return (r == (q % 16) * 16 + q // 16).astype(F32).astype(BF)


def to_token_major():
    r = lax.broadcasted_iota(jnp.int32, (PROWS, ROWS), 0)
    q = lax.broadcasted_iota(jnp.int32, (PROWS, ROWS), 1)
    return (r == (q % 16) * 16 + q // 16).astype(F32).astype(BF)


class Net:
    def __init__(self, send_sem, recv_sem):
        self.send_sem, self.recv_sem = send_sem, recv_sem
        self.started = []

    def send(self, src, dst, device):
        k = len(self.started)
        copy = pltpu.make_async_remote_copy(
            src_ref=src,
            dst_ref=dst,
            send_sem=self.send_sem.at[k],
            recv_sem=self.recv_sem.at[k],
            device_id=device,
            device_id_type=MESH,
        )
        copy.start()
        self.started.append(copy)
        return copy


def row_half(ref, h):
    return ref.at[pl.ds(0, HALF0), :] if h == 0 else ref.at[pl.ds(HALF0, ROWS - HALF0), :]


def lane_half(ref, h):
    return ref.at[:, pl.ds(h * (D // 2), D // 2)]


def kernel(
    tokens, cots, table, comb, w_in, w_down,
    out_ref, back_ref, w_part,
    x_all, cot_send, cot_all, down, bp, ra_opp, ra, rb_opp, rb,
    act_all, wbuf, acc, pgate, pup, grads, ri_opp, ri, rj_opp, rj,
    out_acc, o_send, o_all, out_in, y_send, back_in,
    send_sem, recv_sem, lsem, wsem,
):
    branch = lax.axis_index("branch")
    me = lax.axis_index("mp")
    core = branch % 2
    s_a, s_b = 1 + 3 * core, 4 - 3 * core
    a0, b0 = (me // s_a) % 4, (me // s_b) % 4

    def at(da, db):
        return ((a0 + da + 4) % 4) * s_a + ((b0 + db + 4) % 4) * s_b

    def in_plane(da, db):
        return (branch, at(da, db))

    partner = (branch + 1 - 2 * core, me)
    net = Net(send_sem, recv_sem)

    barrier = pltpu.get_barrier_semaphore()

    def greet_plane(d, _):
        pl.semaphore_signal(barrier, inc=1, device_id=(branch, (me + d) % NM), device_id_type=MESH)
        return 0

    def greet_column(d, _):
        pl.semaphore_signal(barrier, inc=1, device_id=((branch + d) % NB, me), device_id_type=MESH)
        return 0

    lax.fori_loop(1, NM, greet_plane, 0)
    lax.fori_loop(1, NB, greet_column, 0)

    own_down = [
        pltpu.make_async_copy(w_down.at[:, pl.ds(0, MAIN), :], down.at[:, pl.ds(0, MAIN), :], lsem.at[0]),
        pltpu.make_async_copy(w_down.at[:, pl.ds(MAIN, TAIL), :], down.at[:, pl.ds(2 * MAIN, TAIL), :], lsem.at[1]),
    ]
    for c in own_down:
        c.start()

    pick = table[...]
    for g in range(NM):
        cols = slice(g * COLS, (g + 1) * COLS)
        cot_send[g] = dot(pick, cots[:, cols]).astype(BF)
    for g in range(NM):
        cols = slice(g * COLS, (g + 1) * COLS)
        x_all[me, :, cols] = dot(pick, tokens[:, cols]).astype(BF)
    cot_all[me] = cot_send[me]

    pl.semaphore_wait(barrier, NM - 1 + NB - 1)

    cot_copies = []
    for d in range(1, NM):
        to = (me + d) % NM
        cot_copies.append(net.send(cot_send.at[to], cot_all.at[me], (branch, to)))

    def gather_start(buf):
        return {
            "a": [net.send(buf.at[me], buf.at[me], in_plane(1, 0)), net.send(buf.at[me], buf.at[me], in_plane(-1, 0))],
            "b": [[net.send(buf.at[me], buf.at[me], in_plane(0, 1)), net.send(buf.at[me], buf.at[me], in_plane(0, -1))]],
        }

    def gather_a1(buf, st, half):
        st["h"] = []
        for i, da in ((0, -1), (1, 1)):
            st["a"][i].wait_recv()
            blk = buf.at[at(da, 0)]
            st["h"].append(net.send(half(blk, i), half(blk, i), in_plane(-da, 0)))
        for da in (-1, 1):
            blk = buf.at[at(da, 0)]
            st["b"].append([net.send(blk, blk, in_plane(0, 1)), net.send(blk, blk, in_plane(0, -1))])

    def gather_a2(buf, st):
        for h in st["h"]:
            h.wait_recv()
        blk = buf.at[at(2, 0)]
        st["b"].append([net.send(blk, blk, in_plane(0, 1)), net.send(blk, blk, in_plane(0, -1))])
        st["g"] = []

    def gather_b1(buf, st, half, n):
        da = (0, -1, 1, 2)[n]
        pair = []
        for i, db in ((0, -1), (1, 1)):
            st["b"][n][i].wait_recv()
            blk = buf.at[at(da, db)]
            pair.append(net.send(half(blk, i), half(blk, i), in_plane(0, -db)))
        st["g"].append(pair)

    def gather_b2(st, n):
        for g in st["g"][n]:
            g.wait_recv()

    ORDER = (2, 1, -1, 0)

    def reduce_a1(buf, opp, half, st):
        st["o"] = []
        for j, db in enumerate(ORDER):
            blk = buf.at[at(2, db)]
            st["o"].append([net.send(half(blk, 0), half(opp.at[0, j], 0), in_plane(1, 0)),
                            net.send(half(blk, 1), half(opp.at[1, j], 1), in_plane(-1, 0))])

    def reduce_a2(buf, acc_in, half, st):
        st["n"] = []
        for j, db in enumerate(ORDER):
            up, dn = buf.at[at(1, db)], buf.at[at(-1, db)]
            st["n"].append([net.send(half(up, 1), half(acc_in.at[0, j], 1), in_plane(1, 0)),
                            net.send(half(dn, 0), half(acc_in.at[1, j], 0), in_plane(-1, 0))])
        st["m"] = []

    def add_to(dst, src):
        dst[...] = (dst[...].astype(F32) + src[...].astype(F32)).astype(BF)

    def reduce_a3(buf, opp, acc_in, half, st, j):
        db = ORDER[j]
        pair = []
        for i, da in ((0, 1), (1, -1)):
            st["o"][j][i].wait_recv()
            blk = half(buf.at[at(da, db)], i)
            add_to(blk, half(opp.at[i, j], i))
            pair.append(net.send(blk, half(acc_in.at[i, j], i), in_plane(da, 0)))
        st["m"].append(pair)

    def reduce_a4(buf, acc_in, st, j):
        db = ORDER[j]
        for i in (0, 1):
            st["n"][j][i].wait_recv()
            st["m"][j][i].wait_recv()
        blk = buf.at[at(0, db)]
        blk[...] = (blk[...].astype(F32) + acc_in[0, j].astype(F32) + acc_in[1, j].astype(F32)).astype(BF)

    def reduce_b1(buf, opp, half, st):
        blk = buf.at[at(0, 2)]
        st["bo"] = [net.send(half(blk, 0), half(opp.at[0], 0), in_plane(0, 1)),
                    net.send(half(blk, 1), half(opp.at[1], 1), in_plane(0, -1))]

    def reduce_b2(buf, acc_in, half, st):
        up, dn = buf.at[at(0, 1)], buf.at[at(0, -1)]
        st["bn"] = [net.send(half(up, 1), half(acc_in.at[0], 1), in_plane(0, 1)),
                    net.send(half(dn, 0), half(acc_in.at[1], 0), in_plane(0, -1))]

    def reduce_b3(buf, opp, acc_in, half, st):
        st["bm"] = []
        for i, db in ((0, 1), (1, -1)):
            st["bo"][i].wait_recv()
            blk = half(buf.at[at(0, db)], i)
            add_to(blk, half(opp.at[i], i))
            st["bm"].append(net.send(blk, half(acc_in.at[i], i), in_plane(0, db)))

    def reduce_b4(st):
        for i in (0, 1):
            st["bn"][i].wait_recv()
            st["bm"][i].wait_recv()

    toks = gather_start(x_all)
    down_part = [
        net.send(w_down.at[:, pl.ds(0, MAIN), :], down.at[:, pl.ds(MAIN, MAIN), :], partner),
        net.send(w_down.at[:, pl.ds(MAIN, TAIL), :], down.at[:, pl.ds(2 * MAIN + TAIL, TAIL), :], partner),
    ]
    in_part = [net.send(w_in.at[g], w_part.at[g], partner) for g in range(2)]

    for c in cot_copies:
        c.wait_recv()
    cot_rows = dot(to_slot_major(), cot_all[...].reshape(PROWS, COLS)).astype(BF)

    gather_a1(x_all, toks, lane_half)

    for c in own_down:
        c.wait()
    for c in down_part:
        c.wait_recv()

    def partials(da):
        def one(j, _):
            m = at(da, j)
            bp[m] = dot_nt(cot_rows, down[m]).astype(BF)
            return 0

        lax.fori_loop(0, 4, one, 0)

    rs = {}
    partials(2)
    reduce_a1(bp, ra_opp, row_half, rs)
    gather_a2(x_all, toks)
    partials(1)
    partials(-1)
    reduce_a2(bp, ra, row_half, rs)
    for n in range(4):
        gather_b1(x_all, toks, lane_half, n)
    partials(0)
    for j in range(4):
        reduce_a3(bp, ra_opp, ra, row_half, rs, j)
    for n in range(4):
        gather_b2(toks, n)
    for c in in_part:
        c.wait_recv()

    def tiles(i, slot):
        rows = pl.ds(pl.multiple_of(i * KC, KC), KC)
        return [
            pltpu.make_async_copy((w_in if w < 2 else w_part).at[w % 2, rows, :], wbuf.at[slot, w], wsem.at[slot, w])
            for w in range(4)
        ]

    def prime():
        for i in range(WB - 1):
            for c in tiles(i, i):
                c.start()

    def stream(lo, hi, body):
        def one(i, _):
            @pl.when(i + WB - 1 < NK)
            def _():
                for c in tiles(i + WB - 1, (i + WB - 1) % WB):
                    c.start()

            slot = i % WB
            for c in tiles(i, slot):
                c.wait()
            body(i, slot)
            return 0

        lax.fori_loop(lo, hi, one, 0)

    acc[...] = jnp.zeros_like(acc)

    def forward(i, slot):
        cols = pl.ds(pl.multiple_of(i * KC, KC), KC)
        rows = dot(to_slot_major(), x_all[:, :, cols].reshape(PROWS, KC)).astype(BF)
        for w in range(4):
            acc[w] += dot(rows, wbuf[slot, w])

    prime()
    stream(0, 6, forward)
    for j in range(3):
        reduce_a4(bp, ra, rs, j)
        if j == 0:
            reduce_b1(bp, rb_opp, row_half, rs)
    reduce_b2(bp, rb, row_half, rs)
    stream(6, 12, forward)
    reduce_a4(bp, ra, rs, 3)
    reduce_b3(bp, rb_opp, rb, row_half, rs)
    stream(12, NK, forward)

    for dst, w in ((pgate, 0), (pup, 1)):
        dst[:, 0:MAIN] = acc[w, :, 0:MAIN]
        dst[:, MAIN : 2 * MAIN] = acc[w + 2, :, 0:MAIN]
        dst[:, 2 * MAIN : CH] = jnp.concatenate([acc[w, :, MAIN:HID], acc[w + 2, :, MAIN:HID]], axis=1)

    def activate(i, _):
        r = pl.ds(pl.multiple_of(i * 16, 16), 16)
        g = pgate[r, :]
        s = 1.0 / (1.0 + jnp.exp(-g))
        act_all[me, r, :] = (g * s * pup[r, :]).astype(BF)
        return 0

    lax.fori_loop(0, SLOTS, activate, 0)
    acts = gather_start(act_all)

    reduce_b4(rs)

    def gradients(i, _):
        r = pl.ds(pl.multiple_of(i * 16, 16), 16)
        h = bp[me, r, :].astype(F32) + rb[0, r, :].astype(F32) + rb[1, r, :].astype(F32)
        g, u = pgate[r, :], pup[r, :]
        s = 1.0 / (1.0 + jnp.exp(-g))
        pgate[r, :] = h * u * s * (1.0 + g * (1.0 - s))
        pup[r, :] = h * g * s
        return 0

    lax.fori_loop(0, SLOTS, gradients, 0)
    for src, w in ((pgate, 0), (pup, 1)):
        moved = dot(to_token_major(), src[...].astype(BF))
        grads[w, :, 0:MAIN] = moved[:, 0:MAIN].astype(BF)
        grads[w + 2, :, 0:MAIN] = moved[:, MAIN : 2 * MAIN].astype(BF)
        grads[w, :, MAIN:HID] = moved[:, 2 * MAIN : 2 * MAIN + TAIL].astype(BF)
        grads[w + 2, :, MAIN:HID] = moved[:, 2 * MAIN + TAIL : CH].astype(BF)

    gather_a1(act_all, acts, row_half)

    for c in toks["a"] + toks["h"] + sum(toks["b"], []) + sum(toks["g"], []):
        c.wait_send()

    def backward(i, slot):
        cols = pl.ds(pl.multiple_of(i * KC, KC), KC)
        total = dot_nt(grads[0], wbuf[slot, 0])
        for w in range(1, 4):
            total += dot_nt(grads[w], wbuf[slot, w])
        x_all[:, :, cols] = total.astype(BF).reshape(NM, PAD, KC)

    prime()
    stream(0, 6, backward)
    gather_a2(act_all, acts)
    for n in range(2):
        gather_b1(act_all, acts, row_half, n)
    stream(6, 12, backward)
    gather_b1(act_all, acts, row_half, 2)
    stream(12, NK, backward)

    ri_st = {}
    reduce_a1(x_all, ri_opp, lane_half, ri_st)
    reduce_a2(x_all, ri, lane_half, ri_st)
    gather_b1(act_all, acts, row_half, 3)

    def outs(da, db):
        m = at(da, db)
        return dot(act_all[m], down[m])

    out_acc[...] = outs(0, 0)
    for da, db in ((-1, 0), (1, 0), (2, 0)):
        out_acc[...] += outs(da, db)
    for j in range(4):
        reduce_a3(x_all, ri_opp, ri, lane_half, ri_st, j)
    for da in (0, -1, 1, 2):
        for db in (-1, 1):
            out_acc[...] += outs(da, db)
    for j in range(4):
        reduce_a4(x_all, ri, ri_st, j)
        if j == 0:
            reduce_b1(x_all, rj_opp, lane_half, ri_st)
        if j == 2:
            reduce_b2(x_all, rj, lane_half, ri_st)
    for n, da in enumerate((0, -1, 1, 2)):
        gather_b2(acts, n)
        out_acc[...] += outs(da, 2)
    o_send[...] = dot(to_token_major(), out_acc[...].astype(BF)).astype(BF).reshape(NM, PAD, COLS)
    o_all[me] = o_send[me]
    o_copies = []
    for d in range(1, NM):
        to = (me + d) % NM
        o_copies.append(net.send(o_send.at[to], o_all.at[me], (branch, to)))
    reduce_b3(x_all, rj_opp, rj, lane_half, ri_st)
    for c in o_copies:
        c.wait_recv()
    out_in[branch] = o_all[pl.ds(2 * branch, 2)]
    finals = []
    for d in range(1, NB):
        to = (branch + d) % NB
        finals.append(net.send(o_all.at[pl.ds(2 * to, 2)], out_in.at[branch], (to, me)))
    reduce_b4(ri_st)
    for g in range(NB):
        cols = slice(g * OUTC, (g + 1) * OUTC)
        y_send[g] = (
            x_all[me, :, cols].astype(F32) + rj[0, :, cols].astype(F32) + rj[1, :, cols].astype(F32)
        ).astype(BF)
    back_in[branch] = y_send[branch]
    for d in range(1, NB):
        to = (branch + d) % NB
        finals.append(net.send(y_send.at[to], back_in.at[branch], (to, me)))

    weights = comb[...]
    hi = weights.astype(BF)
    lo = (weights - hi.astype(F32)).astype(BF)
    for c in finals[: NB - 1]:
        c.wait_recv()
    for j in range(2):
        got = out_in[:, j].reshape(NB * PAD, COLS)
        out_ref[:, j * COLS : (j + 1) * COLS] = (dot(hi, got) + dot(lo, got)).astype(BF)
    for c in finals[NB - 1 :]:
        c.wait_recv()
    got = back_in[...].reshape(NB * PAD, OUTC)
    back_ref[...] = (dot(hi, got) + dot(lo, got)).astype(BF)

    reused = toks["a"] + toks["h"] + sum(toks["b"], []) + sum(toks["g"], [])
    for c in net.started:
        if not any(c is r for r in reused):
            c.wait_send()


N_COPIES = 200


def on_device(tokens, cotangent, routes, router_gates, expert_in, expert_down):
    branch = lax.axis_index("branch")
    expert, core = branch // 2, branch % 2
    named = routes[:, :, None] == jnp.arange(EXPERTS, dtype=jnp.int32)
    chosen = jnp.any(named, axis=1)
    counted = chosen.astype(jnp.int32)
    places = jnp.cumsum(counted, axis=0) - counted
    mine = jnp.arange(EXPERTS, dtype=jnp.int32) == expert
    own_place = jnp.sum(jnp.where(jnp.logical_and(mine, chosen), places + 1, 0), axis=1) - 1
    spots = jnp.arange(PAD, dtype=jnp.int32)
    wanted = jnp.where(spots < SLOTS, core * SLOTS + spots, -2)
    table = (wanted[:, None] == own_place[None, :]).astype(BF)
    gates = jnp.sum(jnp.where(named, router_gates[:, :, None], 0.0), axis=1)
    column = jnp.arange(NB * PAD, dtype=jnp.int32)
    col_slot = jnp.where(column % PAD < SLOTS, (column // PAD % 2) * SLOTS + column % PAD, -2)
    col_expert = column // (2 * PAD)
    comb = jnp.zeros((TOK, NB * PAD), F32)
    for e in range(EXPERTS):
        hit = jnp.logical_and(col_expert[None, :] == e, col_slot[None, :] == places[:, e : e + 1])
        comb += jnp.where(hit, gates[:, e : e + 1], 0.0)

    vm = pl.BlockSpec(memory_space=pltpu.VMEM)
    hbm = pl.BlockSpec(memory_space=pl.ANY)
    out, back, _ = pl.pallas_call(
        kernel,
        out_shape=(
            jax.ShapeDtypeStruct((TOK, OUTC), BF),
            jax.ShapeDtypeStruct((TOK, OUTC), BF),
            jax.ShapeDtypeStruct((2, D, HID), BF),
        ),
        in_specs=[vm, vm, vm, vm, hbm, hbm],
        out_specs=(vm, vm, hbm),
        scratch_shapes=[
            pltpu.VMEM((NM, PAD, D), BF),
            pltpu.VMEM((NM, PAD, COLS), BF),
            pltpu.VMEM((NM, PAD, COLS), BF),
            pltpu.VMEM((NM, CH, COLS), BF),
            pltpu.VMEM((NM, ROWS, CH), BF),
            pltpu.VMEM((2, 4, ROWS, CH), BF),
            pltpu.VMEM((2, 4, ROWS, CH), BF),
            pltpu.VMEM((2, ROWS, CH), BF),
            pltpu.VMEM((2, ROWS, CH), BF),
            pltpu.VMEM((NM, ROWS, CH), BF),
            pltpu.VMEM((WB, 4, KC, HID), BF),
            pltpu.VMEM((4, ROWS, HID), F32),
            pltpu.VMEM((ROWS, CH), F32),
            pltpu.VMEM((ROWS, CH), F32),
            pltpu.VMEM((4, PROWS, HID), BF),
            pltpu.VMEM((2, 4, PAD, D), BF),
            pltpu.VMEM((2, 4, PAD, D), BF),
            pltpu.VMEM((2, PAD, D), BF),
            pltpu.VMEM((2, PAD, D), BF),
            pltpu.VMEM((ROWS, COLS), F32),
            pltpu.VMEM((NM, PAD, COLS), BF),
            pltpu.VMEM((NM, PAD, COLS), BF),
            pltpu.VMEM((NB, 2, PAD, COLS), BF),
            pltpu.VMEM((NB, PAD, OUTC), BF),
            pltpu.VMEM((NB, PAD, OUTC), BF),
            pltpu.SemaphoreType.DMA((N_COPIES,)),
            pltpu.SemaphoreType.DMA((N_COPIES,)),
            pltpu.SemaphoreType.DMA((2,)),
            pltpu.SemaphoreType.DMA((WB, 4)),
        ],
        compiler_params=pltpu.CompilerParams(
            collective_id=0, has_side_effects=True, vmem_limit_bytes=66060288
        ),
        name="expert_step",
    )(tokens, cotangent, table, comb, expert_in, expert_down.reshape(NM, HID, COLS))
    return out, back


def solution(mesh):
    placed = (
        P("mp", None),
        P("mp", None),
        P("mp", None),
        P("mp", None),
        P(None, None, ("branch", "mp")),
        P("branch", "mp"),
    )
    return jax.shard_map(
        on_device,
        mesh=mesh,
        in_specs=placed,
        out_specs=(P("mp", "branch"), P("mp", "branch")),
        check_vma=False,
    )
```

time: 635 us -> 187 us (0.29)
  blocking collectives: 326 us -> 0 us
  waiting for transfers between devices: 160 us -> 0 us
  Pallas kernels: 0 us -> 158 us
  matrix products: 80.5 us -> 0 us
  between operations: 14.6 us -> 0.7 us
  starting transfers between devices: 12.8 us -> 0 us
  local copies, waits for them, and re-layouts: 34.1 us -> 24.2 us
    unnamed x1 -> x0, blocking collectives: 188 us -> none
    pallas_call x0 -> x1, Pallas kernels: none -> 158 us  [on_device(): pl.pallas_call(kernel, out_shape=(jax.ShapeDtypeStruct((TOK, OUTC), BF),...]
    all_gather x1 -> x0, blocking collectives: 138 us -> none  [on_device(): all_routes = lax.all_gather(routes, 'mp', axis=0, tiled=True)]
    dot_general x8 -> x0, matrix products: 80.5 us -> none  [the longest x3 35.5 us: contract_last(): lax.dot_general(left, right, (((1,), (1,)), ((), ())), preferred_element_...]
    all_gather x2 -> x0, waiting for transfers between devices: 79.2 us -> none  [the longest x1 54.7 us: on_device(): lax.all_gather(cotangent, 'mp', axis=0, tiled=True)]
    reduce_scatter x2 -> x0, waiting for transfers between devices: 65.3 us -> none  [the longest x1 33.2 us: on_device(): lax.psum_scatter(token_in.astype(jnp.bfloat16), 'branch', scatter_dimensi...]
    unnamed x25 -> x3, local copies, waits for them, and re-layouts: 6.66 us -> 23.7 us
    reshape x2 -> x0, local copies, waits for them, and re-layouts: 16 us -> none  [the longest x1 8.05 us: on_device(): inputs = inputs.reshape(shards * CAP, -1)]
  transfers between devices with their start and end apart: 7 -> 0, of which waited for: 6 -> 0; matrix products, arithmetic and copies ran while one was open for 8% -> 0% of each run, Pallas kernels for 0% -> 0%
where the time goes in v1:
time: 187 us; the launch traced here: 186 us
  Pallas kernels  158 us (84%)
  local copies, waits for them, and re-layouts  24.2 us (13%)
  other arithmetic  3.03 us (2%)
    pallas_call x1, Pallas kernels, on_device(): pl.pallas_call(kernel, out_shape=(jax.ShapeDtypeStruct((TOK, OUTC), BF),...  158 us
    unnamed x3, local copies, waits for them, and re-layouts  23.7 us

profile of v1, /device:TPU:1, one launch (start us, length us, event | category | flops | bytes accessed | tf_op | source)
XLA Modules:
  0.0 186.1 jit_solution(15355415139342627692)
XLA Ops:
  0.7 0.7 fusion
  1.4 0.7 select_reduce_fusion.1
  2.1 0.1 copy.14
  2.2 0.1 copy.15
  2.3 0.1 reduce_window_sum.11
  2.4 0.1 select_reduce_fusion
  2.5 0.2 slice_reduce_fusion.3
  2.8 0.7 compare_convert_fusion.table
  3.4 0.7 select_add_fusion.comb
  4.2 20.7 %copy.17.w_in = bf16[2,8192,448]{2,1,0:T(8,128)(2,1)} copy(bf16[2,8192,448]{1,2,0:T(8,128)(2,1)} %param.10) | data formatting | bytes 29360128 | tf_op args[4]
  24.8 158.2 %expert_step.1 = (bf16[48,1024]{1,0:T(8,128)(2,1)}, bf16[48,1024]{1,0:T(8,128)(2,1)}, bf16[2,8192,448]{2,1,0:T(8,128)(2,1)}) custom-call(bf16[48,8192]{1,0:T(8,128)(2,1)} %tokens.1, bf16[48,8192]{1,0:T(8,128)(2,1)} %cots.1, bf16[16,48]{1,0:T(8,128)(2,1)} %compare_convert_fusion.table, f32[48,128]{1,0:T(8,128)} %select_add_fusion.comb, ...), custom_call_target="tpu_custom_call" | custom-call | tf_op jit(solution)/shard_map/expert_step/pallas_call | solution.py:479
  183.1 1.5 copy.20
  184.6 1.5 copy.21
  (8 shorter events, 0.0 us)

commit v2 on v1

--- a/solution.py
+++ b/solution.py
@@ -17,7 +17,6 @@
 TOK = 48
 D = 8192
 HID = 448
-MAIN, TAIL = 384, 64
 CH = 2 * HID
 SLOTS = 15
 PAD = 16
@@ -83,7 +82,7 @@
     tokens, cots, table, comb, w_in, w_down,
     out_ref, back_ref, w_part,
     x_all, cot_send, cot_all, down, bp, ra_opp, ra, rb_opp, rb,
-    act_all, wbuf, acc, pgate, pup, grads, ri_opp, ri, rj_opp, rj,
+    act_all, wbuf, pgate, pup, grads, ri_opp, ri, rj_opp, rj,
     out_acc, o_send, o_all, out_in, y_send, back_in,
     send_sem, recv_sem, lsem, wsem,
 ):
@@ -115,12 +114,8 @@
     lax.fori_loop(1, NM, greet_plane, 0)
     lax.fori_loop(1, NB, greet_column, 0)
 
-    own_down = [
-        pltpu.make_async_copy(w_down.at[:, pl.ds(0, MAIN), :], down.at[:, pl.ds(0, MAIN), :], lsem.at[0]),
-        pltpu.make_async_copy(w_down.at[:, pl.ds(MAIN, TAIL), :], down.at[:, pl.ds(2 * MAIN, TAIL), :], lsem.at[1]),
-    ]
-    for c in own_down:
-        c.start()
+    own_down = pltpu.make_async_copy(w_down, down.at[:, pl.ds(0, HID), :], lsem)
+    own_down.start()
 
     pick = table[...]
     for g in range(NM):
@@ -236,10 +231,7 @@
             st["bm"][i].wait_recv()
 
     toks = gather_start(x_all)
-    down_part = [
-        net.send(w_down.at[:, pl.ds(0, MAIN), :], down.at[:, pl.ds(MAIN, MAIN), :], partner),
-        net.send(w_down.at[:, pl.ds(MAIN, TAIL), :], down.at[:, pl.ds(2 * MAIN + TAIL, TAIL), :], partner),
-    ]
+    down_part = net.send(w_down, down.at[:, pl.ds(HID, HID), :], partner)
     in_part = [net.send(w_in.at[g], w_part.at[g], partner) for g in range(2)]
 
     for c in cot_copies:
@@ -248,10 +240,8 @@
 
     gather_a1(x_all, toks, lane_half)
 
-    for c in own_down:
-        c.wait()
-    for c in down_part:
-        c.wait_recv()
+    own_down.wait()
+    down_part.wait_recv()
 
     def partials(da):
         def one(j, _):
@@ -279,10 +269,11 @@
         c.wait_recv()
 
     def tiles(i, slot):
-        rows = pl.ds(pl.multiple_of(i * KC, KC), KC)
+        cols = pl.ds(pl.multiple_of(i * KC, KC), KC)
         return [
-            pltpu.make_async_copy((w_in if w < 2 else w_part).at[w % 2, rows, :], wbuf.at[slot, w], wsem.at[slot, w])
-            for w in range(4)
+            pltpu.make_async_copy(src.at[g, :, cols], wbuf.at[slot, g, pl.ds(o * HID, HID), :], wsem.at[slot, g, o])
+            for o, src in enumerate((w_in, w_part))
+            for g in range(2)
         ]
 
     def prime():
@@ -305,13 +296,14 @@
 
         lax.fori_loop(lo, hi, one, 0)
 
-    acc[...] = jnp.zeros_like(acc)
+    pgate[...] = jnp.zeros_like(pgate)
+    pup[...] = jnp.zeros_like(pup)
 
     def forward(i, slot):
         cols = pl.ds(pl.multiple_of(i * KC, KC), KC)
         rows = dot(to_slot_major(), x_all[:, :, cols].reshape(PROWS, KC)).astype(BF)
-        for w in range(4):
-            acc[w] += dot(rows, wbuf[slot, w])
+        pgate[...] += dot_nt(rows, wbuf[slot, 0])
+        pup[...] += dot_nt(rows, wbuf[slot, 1])
 
     prime()
     stream(0, 6, forward)
@@ -325,11 +317,6 @@
     reduce_b3(bp, rb_opp, rb, row_half, rs)
     stream(12, NK, forward)
 
-    for dst, w in ((pgate, 0), (pup, 1)):
-        dst[:, 0:MAIN] = acc[w, :, 0:MAIN]
-        dst[:, MAIN : 2 * MAIN] = acc[w + 2, :, 0:MAIN]
-        dst[:, 2 * MAIN : CH] = jnp.concatenate([acc[w, :, MAIN:HID], acc[w + 2, :, MAIN:HID]], axis=1)
-
     def activate(i, _):
         r = pl.ds(pl.multiple_of(i * 16, 16), 16)
         g = pgate[r, :]
@@ -352,12 +339,8 @@
         return 0
 
     lax.fori_loop(0, SLOTS, gradients, 0)
-    for src, w in ((pgate, 0), (pup, 1)):
-        moved = dot(to_token_major(), src[...].astype(BF))
-        grads[w, :, 0:MAIN] = moved[:, 0:MAIN].astype(BF)
-        grads[w + 2, :, 0:MAIN] = moved[:, MAIN : 2 * MAIN].astype(BF)
-        grads[w, :, MAIN:HID] = moved[:, 2 * MAIN : 2 * MAIN + TAIL].astype(BF)
-        grads[w + 2, :, MAIN:HID] = moved[:, 2 * MAIN + TAIL : CH].astype(BF)
+    for w, src in enumerate((pgate, pup)):
+        grads[w] = dot(to_token_major(), src[...].astype(BF)).astype(BF)
 
     gather_a1(act_all, acts, row_half)
 
@@ -366,9 +349,7 @@
 
     def backward(i, slot):
         cols = pl.ds(pl.multiple_of(i * KC, KC), KC)
-        total = dot_nt(grads[0], wbuf[slot, 0])
-        for w in range(1, 4):
-            total += dot_nt(grads[w], wbuf[slot, w])
+        total = dot(grads[0], wbuf[slot, 0]) + dot(grads[1], wbuf[slot, 1])
         x_all[:, :, cols] = total.astype(BF).reshape(NM, PAD, KC)
 
     prime()
@@ -481,7 +462,7 @@
         out_shape=(
             jax.ShapeDtypeStruct((TOK, OUTC), BF),
             jax.ShapeDtypeStruct((TOK, OUTC), BF),
-            jax.ShapeDtypeStruct((2, D, HID), BF),
+            jax.ShapeDtypeStruct((2, HID, D), BF),
         ),
         in_specs=[vm, vm, vm, vm, hbm, hbm],
         out_specs=(vm, vm, hbm),
@@ -496,11 +477,10 @@
             pltpu.VMEM((2, ROWS, CH), BF),
             pltpu.VMEM((2, ROWS, CH), BF),
             pltpu.VMEM((NM, ROWS, CH), BF),
-            pltpu.VMEM((WB, 4, KC, HID), BF),
-            pltpu.VMEM((4, ROWS, HID), F32),
+            pltpu.VMEM((WB, 2, CH, KC), BF),
             pltpu.VMEM((ROWS, CH), F32),
             pltpu.VMEM((ROWS, CH), F32),
-            pltpu.VMEM((4, PROWS, HID), BF),
+            pltpu.VMEM((2, PROWS, CH), BF),
             pltpu.VMEM((2, 4, PAD, D), BF),
             pltpu.VMEM((2, 4, PAD, D), BF),
             pltpu.VMEM((2, PAD, D), BF),
@@ -513,14 +493,14 @@
             pltpu.VMEM((NB, PAD, OUTC), BF),
             pltpu.SemaphoreType.DMA((N_COPIES,)),
             pltpu.SemaphoreType.DMA((N_COPIES,)),
-            pltpu.SemaphoreType.DMA((2,)),
-            pltpu.SemaphoreType.DMA((WB, 4)),
+            pltpu.SemaphoreType.DMA,
+            pltpu.SemaphoreType.DMA((WB, 2, 2)),
         ],
         compiler_params=pltpu.CompilerParams(
             collective_id=0, has_side_effects=True, vmem_limit_bytes=66060288
         ),
         name="expert_step",
-    )(tokens, cotangent, table, comb, expert_in, expert_down.reshape(NM, HID, COLS))
+    )(tokens, cotangent, table, comb, expert_in.transpose(0, 2, 1), expert_down.reshape(NM, HID, COLS))
     return out, back
 
 

time: 187 us -> 166 us (0.89)
  local copies, waits for them, and re-layouts: 24.2 us -> 3.51 us
    unnamed x3 -> x2, local copies, waits for them, and re-layouts: 23.7 us -> 3.08 us
where the time goes in v2:
time: 166 us
  Pallas kernels  158 us (95%)
  local copies, waits for them, and re-layouts  3.51 us (2%)
  other arithmetic  3.03 us (2%)
    pallas_call x1, Pallas kernels, on_device(): pl.pallas_call(kernel, out_shape=(jax.ShapeDtypeStruct((TOK, OUTC), BF),...  158 us

profile of v2, /device:TPU:1, one launch (start us, length us, event | category | flops | bytes accessed | tf_op | source)
XLA Modules:
  0.0 165.7 jit_solution(9345660167844782025)
XLA Ops:
  0.7 0.7 fusion
  1.4 0.7 select_reduce_fusion.1
  2.1 0.1 copy.12
  2.2 0.1 copy.13
  2.3 0.1 reduce_window_sum.11
  2.4 0.1 select_reduce_fusion
  2.5 0.2 slice_reduce_fusion.3
  2.8 0.7 compare_convert_fusion.table
  3.4 0.7 select_add_fusion.comb
  4.2 158.4 %expert_step.1 = (bf16[48,1024]{1,0:T(8,128)(2,1)}, bf16[48,1024]{1,0:T(8,128)(2,1)}, bf16[2,448,8192]{2,1,0:T(8,128)(2,1)}) custom-call(bf16[48,8192]{1,0:T(8,128)(2,1)} %tokens.1, bf16[48,8192]{1,0:T(8,128)(2,1)} %cots.1, bf16[16,48]{1,0:T(8,128)(2,1)} %compare_convert_fusion.table, f32[48,128]{1,0:T(8,128)} %select_add_fusion.comb, ...), custom_call_target="tpu_custom_call" | custom-call | tf_op jit(solution)/shard_map/expert_step/pallas_call | solution.py:460
  162.6 1.5 copy.17
  164.1 1.5 copy.18
  (8 shorter events, 0.0 us)

commit v3 on v2

--- a/solution.py
+++ b/solution.py
@@ -24,9 +24,9 @@
 PROWS = PAD * NM
 COLS = D // NM
 OUTC = D // NB
-KC = 512
+KC = 1024
 NK = D // KC
-WB = 3
+WB = 2
 HALF0 = 128
 
 
@@ -74,16 +74,20 @@
     return ref.at[pl.ds(0, HALF0), :] if h == 0 else ref.at[pl.ds(HALF0, ROWS - HALF0), :]
 
 
+def whole(ref):
+    return ref
+
+
 def lane_half(ref, h):
     return ref.at[:, pl.ds(h * (D // 2), D // 2)]
 
 
 def kernel(
-    tokens, cots, table, comb, w_in, w_down,
+    tokens, cots, routes, gates, w_in, w_down,
     out_ref, back_ref, w_part,
     x_all, cot_send, cot_all, down, bp, ra_opp, ra, rb_opp, rb,
     act_all, wbuf, pgate, pup, grads, ri_opp, ri, rj_opp, rj,
-    out_acc, o_send, o_all, out_in, y_send, back_in,
+    out_acc, o_send, o_all, out_in, y_send, back_in, comb,
     send_sem, recv_sem, lsem, wsem,
 ):
     branch = lax.axis_index("branch")
@@ -117,7 +121,17 @@
     own_down = pltpu.make_async_copy(w_down, down.at[:, pl.ds(0, HID), :], lsem)
     own_down.start()
 
-    pick = table[...]
+    row = lax.broadcasted_iota(jnp.int32, (EXPERTS, TOK), 0)
+    named = [routes[k : k + 1, :] == row for k in range(2)]
+    chosen = jnp.logical_or(named[0], named[1]).astype(F32)
+    earlier = lax.broadcasted_iota(jnp.int32, (TOK, TOK), 0) < lax.broadcasted_iota(jnp.int32, (TOK, TOK), 1)
+    places = dot(chosen.astype(BF), earlier.astype(F32).astype(BF))
+    weight = sum(jnp.where(named[k], gates[k : k + 1, :], 0.0) for k in range(2))
+    own_place = jnp.sum(jnp.where(row == branch // 2, jnp.where(chosen > 0, places, -4.0), 0.0), axis=0, keepdims=True)
+    spot = lax.broadcasted_iota(jnp.int32, (PAD, TOK), 0)
+    wanted = jnp.where(spot < SLOTS, core * SLOTS + spot, -2).astype(F32)
+    pick = (wanted == own_place).astype(F32).astype(BF)
+
     for g in range(NM):
         cols = slice(g * COLS, (g + 1) * COLS)
         cot_send[g] = dot(pick, cots[:, cols]).astype(BF)
@@ -148,21 +162,21 @@
         for da in (-1, 1):
             blk = buf.at[at(da, 0)]
             st["b"].append([net.send(blk, blk, in_plane(0, 1)), net.send(blk, blk, in_plane(0, -1))])
+        st["g"] = []
 
     def gather_a2(buf, st):
         for h in st["h"]:
             h.wait_recv()
         blk = buf.at[at(2, 0)]
         st["b"].append([net.send(blk, blk, in_plane(0, 1)), net.send(blk, blk, in_plane(0, -1))])
-        st["g"] = []
 
     def gather_b1(buf, st, half, n):
         da = (0, -1, 1, 2)[n]
         pair = []
         for i, db in ((0, -1), (1, 1)):
             st["b"][n][i].wait_recv()
-            blk = buf.at[at(da, db)]
-            pair.append(net.send(half(blk, i), half(blk, i), in_plane(0, -db)))
+            part = half(buf.at[at(da, db)], i ^ (n & 1))
+            pair.append(net.send(part, part, in_plane(0, -db)))
         st["g"].append(pair)
 
     def gather_b2(st, n):
@@ -172,40 +186,39 @@
     ORDER = (2, 1, -1, 0)
 
     def reduce_a1(buf, opp, half, st):
-        st["o"] = []
+        st["o"], st["n"], st["m"], st["bm"] = [], [], [], []
         for j, db in enumerate(ORDER):
-            blk = buf.at[at(2, db)]
-            st["o"].append([net.send(half(blk, 0), half(opp.at[0, j], 0), in_plane(1, 0)),
-                            net.send(half(blk, 1), half(opp.at[1, j], 1), in_plane(-1, 0))])
-
-    def reduce_a2(buf, acc_in, half, st):
-        st["n"] = []
-        for j, db in enumerate(ORDER):
+            blk, f = buf.at[at(2, db)], j & 1
+            st["o"].append([net.send(half(blk, f), half(opp.at[0, j], f), in_plane(1, 0)),
+                            net.send(half(blk, 1 - f), half(opp.at[1, j], 1 - f), in_plane(-1, 0))])
+
+    def reduce_a2(buf, acc_in, half, st, js=range(4)):
+        for j in js:
+            db, f = ORDER[j], j & 1
             up, dn = buf.at[at(1, db)], buf.at[at(-1, db)]
-            st["n"].append([net.send(half(up, 1), half(acc_in.at[0, j], 1), in_plane(1, 0)),
-                            net.send(half(dn, 0), half(acc_in.at[1, j], 0), in_plane(-1, 0))])
-        st["m"] = []
+            st["n"].append([net.send(half(up, 1 - f), half(acc_in.at[0, j], 1 - f), in_plane(1, 0)),
+                            net.send(half(dn, f), half(acc_in.at[1, j], f), in_plane(-1, 0))])
 
     def add_to(dst, src):
         dst[...] = (dst[...].astype(F32) + src[...].astype(F32)).astype(BF)
 
     def reduce_a3(buf, opp, acc_in, half, st, j):
-        db = ORDER[j]
+        db, f = ORDER[j], j & 1
         pair = []
         for i, da in ((0, 1), (1, -1)):
             st["o"][j][i].wait_recv()
-            blk = half(buf.at[at(da, db)], i)
-            add_to(blk, half(opp.at[i, j], i))
-            pair.append(net.send(blk, half(acc_in.at[i, j], i), in_plane(da, 0)))
+            blk = half(buf.at[at(da, db)], i ^ f)
+            add_to(blk, half(opp.at[i, j], i ^ f))
+            pair.append(net.send(blk, half(acc_in.at[i, j], i ^ f), in_plane(da, 0)))
         st["m"].append(pair)
 
-    def reduce_a4(buf, acc_in, st, j):
+    def reduce_a4(buf, acc_in, whole, st, j):
         db = ORDER[j]
         for i in (0, 1):
             st["n"][j][i].wait_recv()
             st["m"][j][i].wait_recv()
-        blk = buf.at[at(0, db)]
-        blk[...] = (blk[...].astype(F32) + acc_in[0, j].astype(F32) + acc_in[1, j].astype(F32)).astype(BF)
+        blk, left, right = whole(buf.at[at(0, db)]), whole(acc_in.at[0, j]), whole(acc_in.at[1, j])
+        blk[...] = (blk[...].astype(F32) + left[...].astype(F32) + right[...].astype(F32)).astype(BF)
 
     def reduce_b1(buf, opp, half, st):
         blk = buf.at[at(0, 2)]
@@ -218,7 +231,6 @@
                     net.send(half(dn, 0), half(acc_in.at[1], 0), in_plane(0, -1))]
 
     def reduce_b3(buf, opp, acc_in, half, st):
-        st["bm"] = []
         for i, db in ((0, 1), (1, -1)):
             st["bo"][i].wait_recv()
             blk = half(buf.at[at(0, db)], i)
@@ -231,19 +243,30 @@
             st["bm"][i].wait_recv()
 
     toks = gather_start(x_all)
-    down_part = net.send(w_down, down.at[:, pl.ds(HID, HID), :], partner)
-    in_part = [net.send(w_in.at[g], w_part.at[g], partner) for g in range(2)]
+    DAS = (2, 1, -1, 0)
+    down_part = {}
+    for da in DAS:
+        down_part[da] = []
+        for j in range(4):
+            m = at(j, da)
+            down_part[da].append(net.send(w_down.at[m], down.at[m, pl.ds(HID, HID), :], partner))
+
+    comb[...] = jnp.zeros_like(comb)
+    spot = lax.broadcasted_iota(jnp.int32, (2 * PAD, TOK), 0)
+    slot = jnp.where(spot % PAD < SLOTS, spot // PAD * SLOTS + spot % PAD, -2).astype(F32)
+    for e in range(EXPERTS):
+        rows = slice(2 * PAD * e, 2 * PAD * (e + 1))
+        comb[rows, 0:TOK] = jnp.where(slot == places[e : e + 1, :], weight[e : e + 1, :], 0.0)
 
     for c in cot_copies:
         c.wait_recv()
     cot_rows = dot(to_slot_major(), cot_all[...].reshape(PROWS, COLS)).astype(BF)
-
-    gather_a1(x_all, toks, lane_half)
-
     own_down.wait()
-    down_part.wait_recv()
 
     def partials(da):
+        for c in down_part[da]:
+            c.wait_recv()
+
         def one(j, _):
             m = at(da, j)
             bp[m] = dot_nt(cot_rows, down[m]).astype(BF)
@@ -254,18 +277,26 @@
     rs = {}
     partials(2)
     reduce_a1(bp, ra_opp, row_half, rs)
-    gather_a2(x_all, toks)
+    gather_a1(x_all, toks, lane_half)
     partials(1)
     partials(-1)
-    reduce_a2(bp, ra, row_half, rs)
-    for n in range(4):
-        gather_b1(x_all, toks, lane_half, n)
+    in_part = []
+    for i in range(NK):
+        cols = pl.ds(i * KC, KC)
+        in_part.append([net.send(w_in.at[g, :, cols], w_part.at[g, :, cols], partner) for g in range(2)])
+    gather_b1(x_all, toks, lane_half, 0)
+    gather_a2(x_all, toks)
     partials(0)
+    gather_b1(x_all, toks, lane_half, 1)
+    reduce_a2(bp, ra, row_half, rs, (0, 1))
+    gather_b1(x_all, toks, lane_half, 2)
+    gather_b1(x_all, toks, lane_half, 3)
+    reduce_a2(bp, ra, row_half, rs, (2, 3))
     for j in range(4):
         reduce_a3(bp, ra_opp, ra, row_half, rs, j)
     for n in range(4):
         gather_b2(toks, n)
-    for c in in_part:
+    for c in sum(in_part, []):
         c.wait_recv()
 
     def tiles(i, slot):
@@ -306,16 +337,10 @@
         pup[...] += dot_nt(rows, wbuf[slot, 1])
 
     prime()
-    stream(0, 6, forward)
-    for j in range(3):
-        reduce_a4(bp, ra, rs, j)
-        if j == 0:
-            reduce_b1(bp, rb_opp, row_half, rs)
-    reduce_b2(bp, rb, row_half, rs)
-    stream(6, 12, forward)
-    reduce_a4(bp, ra, rs, 3)
-    reduce_b3(bp, rb_opp, rb, row_half, rs)
-    stream(12, NK, forward)
+    stream(0, 5, forward)
+    reduce_a4(bp, ra, whole, rs, 0)
+    reduce_b1(bp, rb_opp, row_half, rs)
+    stream(5, NK, forward)
 
     def activate(i, _):
         r = pl.ds(pl.multiple_of(i * 16, 16), 16)
@@ -327,6 +352,12 @@
     lax.fori_loop(0, SLOTS, activate, 0)
     acts = gather_start(act_all)
 
+    reduce_a4(bp, ra, whole, rs, 1)
+    reduce_a4(bp, ra, whole, rs, 2)
+    reduce_b2(bp, rb, row_half, rs)
+    reduce_b3(bp, rb_opp, rb, row_half, rs)
+    reduce_a4(bp, ra, whole, rs, 3)
+    gather_a1(act_all, acts, row_half)
     reduce_b4(rs)
 
     def gradients(i, _):
@@ -342,8 +373,6 @@
     for w, src in enumerate((pgate, pup)):
         grads[w] = dot(to_token_major(), src[...].astype(BF)).astype(BF)
 
-    gather_a1(act_all, acts, row_half)
-
     for c in toks["a"] + toks["h"] + sum(toks["b"], []) + sum(toks["g"], []):
         c.wait_send()
 
@@ -352,18 +381,29 @@
         total = dot(grads[0], wbuf[slot, 0]) + dot(grads[1], wbuf[slot, 1])
         x_all[:, :, cols] = total.astype(BF).reshape(NM, PAD, KC)
 
+    def quarter(q):
+        return lambda ref, h: ref.at[:, pl.ds(q * (D // 2) + h * (D // 4), D // 4)]
+
+    def half_of(q):
+        return lambda ref: ref.at[:, pl.ds(q * (D // 2), D // 2)]
+
+    ri_st = [{}, {}]
+
+    def launch(q):
+        reduce_a1(x_all, ri_opp, quarter(q), ri_st[q])
+        reduce_a2(x_all, ri, quarter(q), ri_st[q])
+
     prime()
-    stream(0, 6, backward)
+    stream(0, 2, backward)
     gather_a2(act_all, acts)
-    for n in range(2):
-        gather_b1(act_all, acts, row_half, n)
-    stream(6, 12, backward)
+    gather_b1(act_all, acts, row_half, 0)
+    stream(2, 4, backward)
+    launch(0)
+    gather_b1(act_all, acts, row_half, 1)
+    stream(4, 6, backward)
     gather_b1(act_all, acts, row_half, 2)
-    stream(12, NK, backward)
-
-    ri_st = {}
-    reduce_a1(x_all, ri_opp, lane_half, ri_st)
-    reduce_a2(x_all, ri, lane_half, ri_st)
+    stream(6, NK, backward)
+    launch(1)
     gather_b1(act_all, acts, row_half, 3)
 
     def outs(da, db):
@@ -374,16 +414,18 @@
     for da, db in ((-1, 0), (1, 0), (2, 0)):
         out_acc[...] += outs(da, db)
     for j in range(4):
-        reduce_a3(x_all, ri_opp, ri, lane_half, ri_st, j)
+        reduce_a3(x_all, ri_opp, ri, quarter(0), ri_st[0], j)
     for da in (0, -1, 1, 2):
         for db in (-1, 1):
             out_acc[...] += outs(da, db)
     for j in range(4):
-        reduce_a4(x_all, ri, ri_st, j)
+        reduce_a3(x_all, ri_opp, ri, quarter(1), ri_st[1], j)
+    for j in range(4):
+        reduce_a4(x_all, ri, half_of(0), ri_st[0], j)
         if j == 0:
-            reduce_b1(x_all, rj_opp, lane_half, ri_st)
+            reduce_b1(x_all, rj_opp, quarter(0), ri_st[0])
         if j == 2:
-            reduce_b2(x_all, rj, lane_half, ri_st)
+            reduce_b2(x_all, rj, quarter(0), ri_st[0])
     for n, da in enumerate((0, -1, 1, 2)):
         gather_b2(acts, n)
         out_acc[...] += outs(da, 2)
@@ -393,7 +435,14 @@
     for d in range(1, NM):
         to = (me + d) % NM
         o_copies.append(net.send(o_send.at[to], o_all.at[me], (branch, to)))
-    reduce_b3(x_all, rj_opp, rj, lane_half, ri_st)
+    for j in range(4):
+        reduce_a4(x_all, ri, half_of(1), ri_st[1], j)
+        if j == 0:
+            reduce_b1(x_all, rj_opp, quarter(1), ri_st[1])
+        if j == 2:
+            reduce_b2(x_all, rj, quarter(1), ri_st[1])
+    for q in range(2):
+        reduce_b3(x_all, rj_opp, rj, quarter(q), ri_st[q])
     for c in o_copies:
         c.wait_recv()
     out_in[branch] = o_all[pl.ds(2 * branch, 2)]
@@ -401,8 +450,9 @@
     for d in range(1, NB):
         to = (branch + d) % NB
         finals.append(net.send(o_all.at[pl.ds(2 * to, 2)], out_in.at[branch], (to, me)))
-    reduce_b4(ri_st)
     for g in range(NB):
+        if g % 4 == 0:
+            reduce_b4(ri_st[g // 4])
         cols = slice(g * OUTC, (g + 1) * OUTC)
         y_send[g] = (
             x_all[me, :, cols].astype(F32) + rj[0, :, cols].astype(F32) + rj[1, :, cols].astype(F32)
@@ -412,7 +462,7 @@
         to = (branch + d) % NB
         finals.append(net.send(y_send.at[to], back_in.at[branch], (to, me)))
 
-    weights = comb[...]
+    weights = comb[...].T[0:TOK, :]
     hi = weights.astype(BF)
     lo = (weights - hi.astype(F32)).astype(BF)
     for c in finals[: NB - 1]:
@@ -431,30 +481,10 @@
             c.wait_send()
 
 
-N_COPIES = 200
+N_COPIES = 240
 
 
 def on_device(tokens, cotangent, routes, router_gates, expert_in, expert_down):
-    branch = lax.axis_index("branch")
-    expert, core = branch // 2, branch % 2
-    named = routes[:, :, None] == jnp.arange(EXPERTS, dtype=jnp.int32)
-    chosen = jnp.any(named, axis=1)
-    counted = chosen.astype(jnp.int32)
-    places = jnp.cumsum(counted, axis=0) - counted
-    mine = jnp.arange(EXPERTS, dtype=jnp.int32) == expert
-    own_place = jnp.sum(jnp.where(jnp.logical_and(mine, chosen), places + 1, 0), axis=1) - 1
-    spots = jnp.arange(PAD, dtype=jnp.int32)
-    wanted = jnp.where(spots < SLOTS, core * SLOTS + spots, -2)
-    table = (wanted[:, None] == own_place[None, :]).astype(BF)
-    gates = jnp.sum(jnp.where(named, router_gates[:, :, None], 0.0), axis=1)
-    column = jnp.arange(NB * PAD, dtype=jnp.int32)
-    col_slot = jnp.where(column % PAD < SLOTS, (column // PAD % 2) * SLOTS + column % PAD, -2)
-    col_expert = column // (2 * PAD)
-    comb = jnp.zeros((TOK, NB * PAD), F32)
-    for e in range(EXPERTS):
-        hit = jnp.logical_and(col_expert[None, :] == e, col_slot[None, :] == places[:, e : e + 1])
-        comb += jnp.where(hit, gates[:, e : e + 1], 0.0)
-
     vm = pl.BlockSpec(memory_space=pltpu.VMEM)
     hbm = pl.BlockSpec(memory_space=pl.ANY)
     out, back, _ = pl.pallas_call(
@@ -491,6 +521,7 @@
             pltpu.VMEM((NB, 2, PAD, COLS), BF),
             pltpu.VMEM((NB, PAD, OUTC), BF),
             pltpu.VMEM((NB, PAD, OUTC), BF),
+            pltpu.VMEM((NB * PAD, 128), F32),
             pltpu.SemaphoreType.DMA((N_COPIES,)),
             pltpu.SemaphoreType.DMA((N_COPIES,)),
             pltpu.SemaphoreType.DMA,
@@ -500,7 +531,7 @@
             collective_id=0, has_side_effects=True, vmem_limit_bytes=66060288
         ),
         name="expert_step",
-    )(tokens, cotangent, table, comb, expert_in.transpose(0, 2, 1), expert_down.reshape(NM, HID, COLS))
+    )(tokens, cotangent, routes.T, router_gates.T, expert_in.transpose(0, 2, 1), expert_down.reshape(NM, HID, COLS))
     return out, back
 
 

time: 166 us -> 151 us (0.910)
  Pallas kernels: 158 us -> 147 us
  other arithmetic: 3.03 us -> 0 us
    pallas_call x1, Pallas kernels: 158 us -> 147 us  [on_device(): pl.pallas_call(kernel, out_shape=(jax.ShapeDtypeStruct((TOK, OUTC), BF),...]
where the time goes in v3:
time: 151 us
  Pallas kernels  147 us (97%)
  local copies, waits for them, and re-layouts  3.08 us (2%)
    pallas_call x1, Pallas kernels, on_device(): pl.pallas_call(kernel, out_shape=(jax.ShapeDtypeStruct((TOK, OUTC), BF),...  147 us
    unnamed x2, local copies, waits for them, and re-layouts  3.08 us

profile of v3, /device:TPU:1, one launch (start us, length us, event | category | flops | bytes accessed | tf_op | source)
XLA Modules:
  0.0 150.8 jit_solution(5601985190320901340)
XLA Ops:
  0.6 147.0 %expert_step.1 = (bf16[48,1024]{1,0:T(8,128)(2,1)}, bf16[48,1024]{1,0:T(8,128)(2,1)}, bf16[2,448,8192]{2,1,0:T(8,128)(2,1)}) custom-call(bf16[48,8192]{1,0:T(8,128)(2,1)} %tokens.1, bf16[48,8192]{1,0:T(8,128)(2,1)} %cots.1, s32[2,48]{1,0:T(2,128)} %bitcast.6, f32[2,48]{1,0:T(2,128)} %bitcast.7, bf16[2,448,8192]{2,1,0:T(8,128)(2,1)} %bitcast.4, ...), custom_call_target="tpu_custom_call" | custom-call | tf_op jit(solution)/shard_map/expert_step/pallas_call | solution.py:490
  147.7 1.5 %copy.10 = bf16[48,1024]{1,0:T(8,128)(2,1)} copy(bf16[48,1024]{1,0:T(8,128)(2,1)} %get-tuple-element.8) | data formatting | bytes 196608
  149.2 1.5 %copy.11 = bf16[48,1024]{1,0:T(8,128)(2,1)} copy(bf16[48,1024]{1,0:T(8,128)(2,1)} %get-tuple-element.9) | data formatting | bytes 196608

commit v4 on v3

--- a/solution.py
+++ b/solution.py
@@ -50,24 +50,34 @@
     return (r == (q % 16) * 16 + q // 16).astype(F32).astype(BF)
 
 
+def wait_bytes(ref, sem):
+    pltpu.make_async_copy(ref, ref, sem).wait()
+
+
+class Flow:
+    def __init__(self, net):
+        self.net, self.sem = net, net.send_sem.at[net.flows]
+        net.flows += 1
+
+
 class Net:
     def __init__(self, send_sem, recv_sem):
         self.send_sem, self.recv_sem = send_sem, recv_sem
-        self.started = []
-
-    def send(self, src, dst, device):
-        k = len(self.started)
-        copy = pltpu.make_async_remote_copy(
+        self.flows = self.groups = 0
+
+    def group(self):
+        self.groups += 1
+        return self.recv_sem.at[self.groups - 1]
+
+    def send(self, flow, group, src, dst, device):
+        pltpu.make_async_remote_copy(
             src_ref=src,
             dst_ref=dst,
-            send_sem=self.send_sem.at[k],
-            recv_sem=self.recv_sem.at[k],
+            send_sem=flow.sem,
+            recv_sem=group,
             device_id=device,
             device_id_type=MESH,
-        )
-        copy.start()
-        self.started.append(copy)
-        return copy
+        ).start()
 
 
 def row_half(ref, h):
@@ -83,11 +93,11 @@
 
 
 def kernel(
-    tokens, cots, routes, gates, w_in, w_down,
+    tokens_hbm, cots_hbm, routes, gates, w_in, w_down,
     out_ref, back_ref, w_part,
     x_all, cot_send, cot_all, down, bp, ra_opp, ra, rb_opp, rb,
     act_all, wbuf, pgate, pup, grads, ri_opp, ri, rj_opp, rj,
-    out_acc, o_send, o_all, out_in, y_send, back_in, comb,
+    out_acc, o_send, o_all, out_in, y_send, back_in, comb, tokens, cots,
     send_sem, recv_sem, lsem, wsem,
 ):
     branch = lax.axis_index("branch")
@@ -118,7 +128,14 @@
     lax.fori_loop(1, NM, greet_plane, 0)
     lax.fori_loop(1, NB, greet_column, 0)
 
-    own_down = pltpu.make_async_copy(w_down, down.at[:, pl.ds(0, HID), :], lsem)
+    loads = [
+        pltpu.make_async_copy(src, dst, lsem.at[i])
+        for i, (src, dst) in enumerate(((cots_hbm, cots), (tokens_hbm, tokens)))
+    ]
+    for c in loads:
+        c.start()
+
+    own_down = pltpu.make_async_copy(w_down, down.at[:, pl.ds(0, HID), :], lsem.at[2])
     own_down.start()
 
     row = lax.broadcasted_iota(jnp.int32, (EXPERTS, TOK), 0)
@@ -132,9 +149,11 @@
     wanted = jnp.where(spot < SLOTS, core * SLOTS + spot, -2).astype(F32)
     pick = (wanted == own_place).astype(F32).astype(BF)
 
+    loads[0].wait()
     for g in range(NM):
         cols = slice(g * COLS, (g + 1) * COLS)
         cot_send[g] = dot(pick, cots[:, cols]).astype(BF)
+    loads[1].wait()
     for g in range(NM):
         cols = slice(g * COLS, (g + 1) * COLS)
         x_all[me, :, cols] = dot(pick, tokens[:, cols]).astype(BF)
@@ -142,114 +161,115 @@
 
     pl.semaphore_wait(barrier, NM - 1 + NB - 1)
 
-    cot_copies = []
+    cot_flow, cot_group = Flow(net), net.group()
     for d in range(1, NM):
         to = (me + d) % NM
-        cot_copies.append(net.send(cot_send.at[to], cot_all.at[me], (branch, to)))
+        net.send(cot_flow, cot_group, cot_send.at[to], cot_all.at[me], (branch, to))
+
+    def both_b(buf, st, da):
+        blk, g = buf.at[at(da, 0)], net.group()
+        for db in (1, -1):
+            net.send(st["flow"], g, blk, blk, in_plane(0, db))
+        st["b"].append(g)
 
     def gather_start(buf):
-        return {
-            "a": [net.send(buf.at[me], buf.at[me], in_plane(1, 0)), net.send(buf.at[me], buf.at[me], in_plane(-1, 0))],
-            "b": [[net.send(buf.at[me], buf.at[me], in_plane(0, 1)), net.send(buf.at[me], buf.at[me], in_plane(0, -1))]],
-        }
+        st = {"flow": Flow(net), "a": net.group(), "b": [], "g": []}
+        for da in (1, -1):
+            net.send(st["flow"], st["a"], buf.at[me], buf.at[me], in_plane(da, 0))
+        both_b(buf, st, 0)
+        return st
 
     def gather_a1(buf, st, half):
-        st["h"] = []
+        wait_bytes(buf.at[pl.ds(0, 2)], st["a"])
+        st["h"] = net.group()
         for i, da in ((0, -1), (1, 1)):
-            st["a"][i].wait_recv()
-            blk = buf.at[at(da, 0)]
-            st["h"].append(net.send(half(blk, i), half(blk, i), in_plane(-da, 0)))
-        for da in (-1, 1):
-            blk = buf.at[at(da, 0)]
-            st["b"].append([net.send(blk, blk, in_plane(0, 1)), net.send(blk, blk, in_plane(0, -1))])
-        st["g"] = []
+            part = half(buf.at[at(da, 0)], i)
+            net.send(st["flow"], st["h"], part, part, in_plane(-da, 0))
+        both_b(buf, st, -1)
+        both_b(buf, st, 1)
 
     def gather_a2(buf, st):
-        for h in st["h"]:
-            h.wait_recv()
-        blk = buf.at[at(2, 0)]
-        st["b"].append([net.send(blk, blk, in_plane(0, 1)), net.send(blk, blk, in_plane(0, -1))])
+        wait_bytes(buf.at[0], st["h"])
+        both_b(buf, st, 2)
 
     def gather_b1(buf, st, half, n):
         da = (0, -1, 1, 2)[n]
-        pair = []
+        wait_bytes(buf.at[pl.ds(0, 2)], st["b"][n])
+        g = net.group()
         for i, db in ((0, -1), (1, 1)):
-            st["b"][n][i].wait_recv()
             part = half(buf.at[at(da, db)], i ^ (n & 1))
-            pair.append(net.send(part, part, in_plane(0, -db)))
-        st["g"].append(pair)
-
-    def gather_b2(st, n):
-        for g in st["g"][n]:
-            g.wait_recv()
+            net.send(st["flow"], g, part, part, in_plane(0, -db))
+        st["g"].append(g)
+
+    def gather_b2(buf, st, n):
+        wait_bytes(buf.at[0], st["g"][n])
+
+    def sent(buf, st):
+        wait_bytes(buf.at[pl.ds(0, NM - 1)], st["flow"].sem)
 
     ORDER = (2, 1, -1, 0)
 
     def reduce_a1(buf, opp, half, st):
-        st["o"], st["n"], st["m"], st["bm"] = [], [], [], []
+        st["o"], st["n"] = [], [net.group() for _ in ORDER]
+        st["bo"], st["bn"] = net.group(), net.group()
         for j, db in enumerate(ORDER):
-            blk, f = buf.at[at(2, db)], j & 1
-            st["o"].append([net.send(half(blk, f), half(opp.at[0, j], f), in_plane(1, 0)),
-                            net.send(half(blk, 1 - f), half(opp.at[1, j], 1 - f), in_plane(-1, 0))])
+            blk, f, g = buf.at[at(2, db)], j & 1, net.group()
+            net.send(st["flow"], g, half(blk, f), half(opp.at[0, j], f), in_plane(1, 0))
+            net.send(st["flow"], g, half(blk, 1 - f), half(opp.at[1, j], 1 - f), in_plane(-1, 0))
+            st["o"].append(g)
 
     def reduce_a2(buf, acc_in, half, st, js=range(4)):
         for j in js:
-            db, f = ORDER[j], j & 1
+            db, f, g = ORDER[j], j & 1, st["n"][j]
             up, dn = buf.at[at(1, db)], buf.at[at(-1, db)]
-            st["n"].append([net.send(half(up, 1 - f), half(acc_in.at[0, j], 1 - f), in_plane(1, 0)),
-                            net.send(half(dn, f), half(acc_in.at[1, j], f), in_plane(-1, 0))])
+            net.send(st["flow"], g, half(up, 1 - f), half(acc_in.at[0, j], 1 - f), in_plane(1, 0))
+            net.send(st["flow"], g, half(dn, f), half(acc_in.at[1, j], f), in_plane(-1, 0))
 
     def add_to(dst, src):
         dst[...] = (dst[...].astype(F32) + src[...].astype(F32)).astype(BF)
 
-    def reduce_a3(buf, opp, acc_in, half, st, j):
+    def reduce_a3(buf, opp, acc_in, half, whole, st, j):
         db, f = ORDER[j], j & 1
-        pair = []
+        wait_bytes(whole(buf.at[0]), st["o"][j])
         for i, da in ((0, 1), (1, -1)):
-            st["o"][j][i].wait_recv()
             blk = half(buf.at[at(da, db)], i ^ f)
             add_to(blk, half(opp.at[i, j], i ^ f))
-            pair.append(net.send(blk, half(acc_in.at[i, j], i ^ f), in_plane(da, 0)))
-        st["m"].append(pair)
+            net.send(st["flow"], st["n"][j], blk, half(acc_in.at[i, j], i ^ f), in_plane(da, 0))
 
     def reduce_a4(buf, acc_in, whole, st, j):
         db = ORDER[j]
-        for i in (0, 1):
-            st["n"][j][i].wait_recv()
-            st["m"][j][i].wait_recv()
+        wait_bytes(whole(acc_in.at[:, j]), st["n"][j])
         blk, left, right = whole(buf.at[at(0, db)]), whole(acc_in.at[0, j]), whole(acc_in.at[1, j])
         blk[...] = (blk[...].astype(F32) + left[...].astype(F32) + right[...].astype(F32)).astype(BF)
 
     def reduce_b1(buf, opp, half, st):
         blk = buf.at[at(0, 2)]
-        st["bo"] = [net.send(half(blk, 0), half(opp.at[0], 0), in_plane(0, 1)),
-                    net.send(half(blk, 1), half(opp.at[1], 1), in_plane(0, -1))]
+        net.send(st["flow"], st["bo"], half(blk, 0), half(opp.at[0], 0), in_plane(0, 1))
+        net.send(st["flow"], st["bo"], half(blk, 1), half(opp.at[1], 1), in_plane(0, -1))
 
     def reduce_b2(buf, acc_in, half, st):
         up, dn = buf.at[at(0, 1)], buf.at[at(0, -1)]
-        st["bn"] = [net.send(half(up, 1), half(acc_in.at[0], 1), in_plane(0, 1)),
-                    net.send(half(dn, 0), half(acc_in.at[1], 0), in_plane(0, -1))]
-
-    def reduce_b3(buf, opp, acc_in, half, st):
+        net.send(st["flow"], st["bn"], half(up, 1), half(acc_in.at[0], 1), in_plane(0, 1))
+        net.send(st["flow"], st["bn"], half(dn, 0), half(acc_in.at[1], 0), in_plane(0, -1))
+
+    def reduce_b3(buf, opp, acc_in, half, whole, st):
+        wait_bytes(whole(buf.at[0]), st["bo"])
         for i, db in ((0, 1), (1, -1)):
-            st["bo"][i].wait_recv()
             blk = half(buf.at[at(0, db)], i)
             add_to(blk, half(opp.at[i], i))
-            st["bm"].append(net.send(blk, half(acc_in.at[i], i), in_plane(0, db)))
-
-    def reduce_b4(st):
-        for i in (0, 1):
-            st["bn"][i].wait_recv()
-            st["bm"][i].wait_recv()
+            net.send(st["flow"], st["bn"], blk, half(acc_in.at[i], i), in_plane(0, db))
+
+    def reduce_b4(acc_in, whole, st):
+        wait_bytes(whole(acc_in), st["bn"])
 
     toks = gather_start(x_all)
     DAS = (2, 1, -1, 0)
-    down_part = {}
+    down_flow, down_part = Flow(net), {}
     for da in DAS:
-        down_part[da] = []
+        down_part[da] = net.group()
         for j in range(4):
             m = at(j, da)
-            down_part[da].append(net.send(w_down.at[m], down.at[m, pl.ds(HID, HID), :], partner))
+            net.send(down_flow, down_part[da], w_down.at[m], down.at[m, pl.ds(HID, HID), :], partner)
 
     comb[...] = jnp.zeros_like(comb)
     spot = lax.broadcasted_iota(jnp.int32, (2 * PAD, TOK), 0)
@@ -258,14 +278,12 @@
         rows = slice(2 * PAD * e, 2 * PAD * (e + 1))
         comb[rows, 0:TOK] = jnp.where(slot == places[e : e + 1, :], weight[e : e + 1, :], 0.0)
 
-    for c in cot_copies:
-        c.wait_recv()
+    wait_bytes(cot_all.at[pl.ds(0, NM - 1)], cot_group)
     cot_rows = dot(to_slot_major(), cot_all[...].reshape(PROWS, COLS)).astype(BF)
     own_down.wait()
 
     def partials(da):
-        for c in down_part[da]:
-            c.wait_recv()
+        wait_bytes(w_down.at[pl.ds(0, 4)], down_part[da])
 
         def one(j, _):
             m = at(da, j)
@@ -274,16 +292,14 @@
 
         lax.fori_loop(0, 4, one, 0)
 
-    rs = {}
+    rs = {"flow": Flow(net)}
     partials(2)
     reduce_a1(bp, ra_opp, row_half, rs)
     gather_a1(x_all, toks, lane_half)
     partials(1)
     partials(-1)
-    in_part = []
-    for i in range(NK):
-        cols = pl.ds(i * KC, KC)
-        in_part.append([net.send(w_in.at[g, :, cols], w_part.at[g, :, cols], partner) for g in range(2)])
+    in_flow, in_group = Flow(net), net.group()
+    net.send(in_flow, in_group, w_in, w_part, partner)
     gather_b1(x_all, toks, lane_half, 0)
     gather_a2(x_all, toks)
     partials(0)
@@ -293,11 +309,10 @@
     gather_b1(x_all, toks, lane_half, 3)
     reduce_a2(bp, ra, row_half, rs, (2, 3))
     for j in range(4):
-        reduce_a3(bp, ra_opp, ra, row_half, rs, j)
+        reduce_a3(bp, ra_opp, ra, row_half, whole, rs, j)
     for n in range(4):
-        gather_b2(toks, n)
-    for c in sum(in_part, []):
-        c.wait_recv()
+        gather_b2(x_all, toks, n)
+    wait_bytes(w_part, in_group)
 
     def tiles(i, slot):
         cols = pl.ds(pl.multiple_of(i * KC, KC), KC)
@@ -355,10 +370,10 @@
     reduce_a4(bp, ra, whole, rs, 1)
     reduce_a4(bp, ra, whole, rs, 2)
     reduce_b2(bp, rb, row_half, rs)
-    reduce_b3(bp, rb_opp, rb, row_half, rs)
+    reduce_b3(bp, rb_opp, rb, row_half, whole, rs)
     reduce_a4(bp, ra, whole, rs, 3)
     gather_a1(act_all, acts, row_half)
-    reduce_b4(rs)
+    reduce_b4(rb, whole, rs)
 
     def gradients(i, _):
         r = pl.ds(pl.multiple_of(i * 16, 16), 16)
@@ -373,8 +388,7 @@
     for w, src in enumerate((pgate, pup)):
         grads[w] = dot(to_token_major(), src[...].astype(BF)).astype(BF)
 
-    for c in toks["a"] + toks["h"] + sum(toks["b"], []) + sum(toks["g"], []):
-        c.wait_send()
+    sent(x_all, toks)
 
     def backward(i, slot):
         cols = pl.ds(pl.multiple_of(i * KC, KC), KC)
@@ -385,9 +399,10 @@
         return lambda ref, h: ref.at[:, pl.ds(q * (D // 2) + h * (D // 4), D // 4)]
 
     def half_of(q):
-        return lambda ref: ref.at[:, pl.ds(q * (D // 2), D // 2)]
-
-    ri_st = [{}, {}]
+        return lambda ref: ref.at[..., pl.ds(q * (D // 2), D // 2)]
+
+    ri_flow = Flow(net)
+    ri_st = [{"flow": ri_flow}, {"flow": ri_flow}]
 
     def launch(q):
         reduce_a1(x_all, ri_opp, quarter(q), ri_st[q])
@@ -414,12 +429,12 @@
     for da, db in ((-1, 0), (1, 0), (2, 0)):
         out_acc[...] += outs(da, db)
     for j in range(4):
-        reduce_a3(x_all, ri_opp, ri, quarter(0), ri_st[0], j)
+        reduce_a3(x_all, ri_opp, ri, quarter(0), half_of(0), ri_st[0], j)
     for da in (0, -1, 1, 2):
         for db in (-1, 1):
             out_acc[...] += outs(da, db)
     for j in range(4):
-        reduce_a3(x_all, ri_opp, ri, quarter(1), ri_st[1], j)
+        reduce_a3(x_all, ri_opp, ri, quarter(1), half_of(1), ri_st[1], j)
     for j in range(4):
         reduce_a4(x_all, ri, half_of(0), ri_st[0], j)
         if j == 0:
@@ -427,14 +442,14 @@
         if j == 2:
             reduce_b2(x_all, rj, quarter(0), ri_st[0])
     for n, da in enumerate((0, -1, 1, 2)):
-        gather_b2(acts, n)
+        gather_b2(act_all, acts, n)
         out_acc[...] += outs(da, 2)
     o_send[...] = dot(to_token_major(), out_acc[...].astype(BF)).astype(BF).reshape(NM, PAD, COLS)
     o_all[me] = o_send[me]
-    o_copies = []
+    o_flow, o_group = Flow(net), net.group()
     for d in range(1, NM):
         to = (me + d) % NM
-        o_copies.append(net.send(o_send.at[to], o_all.at[me], (branch, to)))
+        net.send(o_flow, o_group, o_send.at[to], o_all.at[me], (branch, to))
     for j in range(4):
         reduce_a4(x_all, ri, half_of(1), ri_st[1], j)
         if j == 0:
@@ -442,46 +457,50 @@
         if j == 2:
             reduce_b2(x_all, rj, quarter(1), ri_st[1])
     for q in range(2):
-        reduce_b3(x_all, rj_opp, rj, quarter(q), ri_st[q])
-    for c in o_copies:
-        c.wait_recv()
+        reduce_b3(x_all, rj_opp, rj, quarter(q), half_of(q), ri_st[q])
+    wait_bytes(o_all.at[pl.ds(0, NM - 1)], o_group)
     out_in[branch] = o_all[pl.ds(2 * branch, 2)]
-    finals = []
+    out_flow, out_group = Flow(net), net.group()
     for d in range(1, NB):
         to = (branch + d) % NB
-        finals.append(net.send(o_all.at[pl.ds(2 * to, 2)], out_in.at[branch], (to, me)))
+        net.send(out_flow, out_group, o_all.at[pl.ds(2 * to, 2)], out_in.at[branch], (to, me))
     for g in range(NB):
         if g % 4 == 0:
-            reduce_b4(ri_st[g // 4])
+            reduce_b4(rj, half_of(g // 4), ri_st[g // 4])
         cols = slice(g * OUTC, (g + 1) * OUTC)
         y_send[g] = (
             x_all[me, :, cols].astype(F32) + rj[0, :, cols].astype(F32) + rj[1, :, cols].astype(F32)
         ).astype(BF)
     back_in[branch] = y_send[branch]
+    back_flow, back_group = Flow(net), net.group()
     for d in range(1, NB):
         to = (branch + d) % NB
-        finals.append(net.send(y_send.at[to], back_in.at[branch], (to, me)))
+        net.send(back_flow, back_group, y_send.at[to], back_in.at[branch], (to, me))
 
     weights = comb[...].T[0:TOK, :]
     hi = weights.astype(BF)
     lo = (weights - hi.astype(F32)).astype(BF)
-    for c in finals[: NB - 1]:
-        c.wait_recv()
+    wait_bytes(out_in.at[pl.ds(0, NB - 1)], out_group)
     for j in range(2):
         got = out_in[:, j].reshape(NB * PAD, COLS)
         out_ref[:, j * COLS : (j + 1) * COLS] = (dot(hi, got) + dot(lo, got)).astype(BF)
-    for c in finals[NB - 1 :]:
-        c.wait_recv()
+    wait_bytes(back_in.at[pl.ds(0, NB - 1)], back_group)
     got = back_in[...].reshape(NB * PAD, OUTC)
     back_ref[...] = (dot(hi, got) + dot(lo, got)).astype(BF)
 
-    reused = toks["a"] + toks["h"] + sum(toks["b"], []) + sum(toks["g"], [])
-    for c in net.started:
-        if not any(c is r for r in reused):
-            c.wait_send()
-
-
-N_COPIES = 240
+    wait_bytes(cot_send.at[pl.ds(0, NM - 1)], cot_flow.sem)
+    wait_bytes(w_down, down_flow.sem)
+    wait_bytes(w_in, in_flow.sem)
+    sent(bp, rs)
+    sent(act_all, acts)
+    sent(x_all, ri_st[0])
+    wait_bytes(o_send.at[pl.ds(0, NM - 1)], o_flow.sem)
+    wait_bytes(out_in.at[pl.ds(0, NB - 1)], out_flow.sem)
+    wait_bytes(back_in.at[pl.ds(0, NB - 1)], back_flow.sem)
+    assert net.flows == N_FLOWS and net.groups == N_GROUPS, (net.flows, net.groups)
+
+
+N_FLOWS, N_GROUPS = 10, 59
 
 
 def on_device(tokens, cotangent, routes, router_gates, expert_in, expert_down):
@@ -494,7 +513,7 @@
             jax.ShapeDtypeStruct((TOK, OUTC), BF),
             jax.ShapeDtypeStruct((2, HID, D), BF),
         ),
-        in_specs=[vm, vm, vm, vm, hbm, hbm],
+        in_specs=[hbm, hbm, vm, vm, hbm, hbm],
         out_specs=(vm, vm, hbm),
         scratch_shapes=[
             pltpu.VMEM((NM, PAD, D), BF),
@@ -522,9 +541,11 @@
             pltpu.VMEM((NB, PAD, OUTC), BF),
             pltpu.VMEM((NB, PAD, OUTC), BF),
             pltpu.VMEM((NB * PAD, 128), F32),
-            pltpu.SemaphoreType.DMA((N_COPIES,)),
-            pltpu.SemaphoreType.DMA((N_COPIES,)),
-            pltpu.SemaphoreType.DMA,
+            pltpu.VMEM((TOK, D), BF),
+            pltpu.VMEM((TOK, D), BF),
+            pltpu.SemaphoreType.DMA((N_FLOWS,)),
+            pltpu.SemaphoreType.DMA((N_GROUPS,)),
+            pltpu.SemaphoreType.DMA((3,)),
             pltpu.SemaphoreType.DMA((WB, 2, 2)),
         ],
         compiler_params=pltpu.CompilerParams(

time: 151 us -> 147 us (0.974)
  Pallas kernels: 147 us -> 143 us
    pallas_call x1, Pallas kernels: 147 us -> 143 us  [on_device(): pl.pallas_call(kernel, out_shape=(jax.ShapeDtypeStruct((TOK, OUTC), BF),...]
where the time goes in v4:
time: 147 us; the launch traced here: 146 us
  Pallas kernels  143 us (97%)
  local copies, waits for them, and re-layouts  3.08 us (2%)
    pallas_call x1, Pallas kernels, on_device(): pl.pallas_call(kernel, out_shape=(jax.ShapeDtypeStruct((TOK, OUTC), BF),...  143 us
    unnamed x2, local copies, waits for them, and re-layouts  3.08 us

profile of v4, /device:TPU:1, one launch (start us, length us, event | category | flops | bytes accessed | tf_op | source)
XLA Modules:
  0.0 146.5 jit_solution(17346619981777354062)
XLA Ops:
  0.6 142.8 %expert_step.1 = (bf16[48,1024]{1,0:T(8,128)(2,1)}, bf16[48,1024]{1,0:T(8,128)(2,1)}, bf16[2,448,8192]{2,1,0:T(8,128)(2,1)}) custom-call(bf16[48,8192]{1,0:T(8,128)(2,1)} %tokens_hbm.1, bf16[48,8192]{1,0:T(8,128)(2,1)} %cots_hbm.1, s32[2,48]{1,0:T(2,128)} %bitcast.6, f32[2,48]{1,0:T(2,128)} %bitcast.7, bf16[2,448,8192]{2,1,0:T(8,128)(2,1)} %bitcast.4, ...), custom_call_target="tpu_custom_call" | custom-call | tf_op jit(solution)/shard_map/expert_step/pallas_call | solution.py:509
  143.4 1.5 %copy.10 = bf16[48,1024]{1,0:T(8,128)(2,1)} copy(bf16[48,1024]{1,0:T(8,128)(2,1)} %get-tuple-element.8) | data formatting | bytes 196608
  144.9 1.5 %copy.11 = bf16[48,1024]{1,0:T(8,128)(2,1)} copy(bf16[48,1024]{1,0:T(8,128)(2,1)} %get-tuple-element.9) | data formatting | bytes 196608
